TPU v7x, 128 devices: a whole 4x4x4 slice. The times are simulated.
128 devices in a mesh: shot: 16 (over x_hi, y, core), tile: 8 (over z, x_lo).
Axes of the slice: x: 4 (x_hi: 2, x_lo: 2; x = x_hi * 2 + x_lo), y: 4, z: 4, core: 2. Of those that a mesh axis runs over, the one named last changes fastest.
Arguments:
- courant: float32 [256, 256, 128], P('shot', 'tile'), may hold values from 0.03 to 0.18
- damping: float32 [256, 256, 128], P('shot', 'tile'), may hold values from 0.02 to 0.3
- aperture_block: int32 [16], replicated, may hold values from 0 to 10
- source_cell: int32 [16], P('shot'), may hold values from 0 to 3145727
- receiver_depth: int32 [16], P('shot'), may hold values from 0 to 127
- wavelet: float32 [16, 8], P('shot'), may hold values from -48 to 48
- receiver_data: float32 [16, 8, 96, 256], P('shot', None, None, 'tile'), may hold values from -6 to 6
- forward_state: float32 [16, 2, 96, 256, 128], P('shot', None, None, 'tile'), may hold values from -6 to 6
- adjoint_state: float32 [16, 2, 96, 256, 128], P('shot', None, None, 'tile'), may hold values from -6 to 6
Outputs:
- image: float32 [256, 256, 128], P('shot', 'tile')
Inputs may be any that keep to these rules, and one draw needn't show every extreme that they name: Shot s's aperture covers model indices 16 * aperture_block[s] to 16 * aperture_block[s] + 95 of dimension 0. `source_cell`: decodes as x * 96 * 128 + y * 128 + z in aperture coordinates.
All inputs are finite; a program needn't handle non-finite values.
Results may differ from a plain program's by a relative error of at most 0.0003.
Values sent between devices are 32-bit elements; how exact they have to be, the bound alone decides.
A program may use at most 128 MiB of HBM per device.

v0:
```python
import jax
import jax.numpy as jnp
from jax import lax
from jax.sharding import PartitionSpec as P

STENCIL_WEIGHTS = (-205.0 / 72.0, 8.0 / 5.0, -1.0 / 5.0, 8.0 / 315.0, -1.0 / 560.0)


def padded_2(cells, sides, width):
    for axis, dim in sides:
        count = lax.axis_size(axis)
        ends = count - 1
        head = lax.slice_in_dim(cells, 0, width, axis=dim)
        tail = lax.slice_in_dim(cells, cells.shape[dim] - width, cells.shape[dim], axis=dim)
        cells = jnp.concatenate(
            [
                lax.ppermute(tail, axis, [(i, (i + 1) % count) for i in range(ends)]),
                cells,
                lax.ppermute(head, axis, [((i + 1) % count, i) for i in range(ends)]),
            ],
            axis=dim,
        )
    return cells


def laplace_local(padded):
    width = padded.shape[1] - 8
    core = padded[:, 4 : 4 + width, :]
    framed = jnp.pad(core, ((4, 4), (0, 0), (4, 4)))
    first = core.shape[0]
    third = core.shape[2]
    total = 3.0 * STENCIL_WEIGHTS[0] * core
    for offset in range(1, 5):
        near = (
            framed[4 + offset : 4 + offset + first, :, 4 : 4 + third]
            + framed[4 - offset : 4 - offset + first, :, 4 : 4 + third]
        )
        near = (
            near
            + padded[:, 4 + offset : 4 + offset + width, :]
            + padded[:, 4 - offset : 4 - offset + width, :]
        )
        near = (
            near
            + framed[4 : 4 + first, :, 4 + offset : 4 + offset + third]
            + framed[4 : 4 + first, :, 4 - offset : 4 - offset + third]
        )
        total = total + STENCIL_WEIGHTS[offset] * near
    return total


def update(padded, previous, speed, absorb, forcing):
    width = padded.shape[1] - 8
    current = padded[:, 4 : 4 + width, :]
    return (2.0 * current - (1.0 - absorb) * previous + speed * laplace_local(padded) + forcing) / (
        1.0 + absorb
    )


def body(
    courant,
    damping,
    aperture_block,
    source_cell,
    receiver_depth,
    wavelet,
    receiver_data,
    forward_state,
    adjoint_state,
):
    block_rows = courant.shape[0]
    local_x = courant.shape[1]
    depth_cells = courant.shape[2]
    span_y = forward_state.shape[2]
    member = lax.axis_index("shot")
    first_row = aperture_block[member] * block_rows
    piece = (
        lax.all_gather(courant, "shot", axis=0, tiled=True),
        lax.all_gather(damping, "shot", axis=0, tiled=True),
    )
    count = piece[0].shape[0]
    wanted = jnp.arange(span_y, dtype=jnp.int32) + first_row
    valid = ((wanted >= 0) & (wanted < count))[:, None, None]
    safe = jnp.clip(wanted, 0, count - 1)
    speed = jnp.where(valid, jnp.take(piece[0], safe, axis=0), 0.0)
    absorb = jnp.where(valid, jnp.take(piece[1], safe, axis=0), 0.0)
    offset_x = lax.axis_index("tile") * local_x
    index_y = jnp.arange(span_y, dtype=jnp.int32).reshape(-1, 1, 1)
    index_z = jnp.arange(depth_cells, dtype=jnp.int32).reshape(1, 1, -1)
    cell = source_cell[0]
    source_x = cell // (span_y * depth_cells)
    source_y = cell // depth_cells % span_y
    source_z = cell % depth_cells
    plane = (index_z == receiver_depth[0]).astype(jnp.float32)
    steps_count = wavelet.shape[1]
    zeros_field = jnp.zeros((span_y, local_x, depth_cells), jnp.float32)
    index_x = jnp.arange(local_x, dtype=jnp.int32).reshape(1, -1, 1) + offset_x
    source = ((index_y == source_y) & (index_x == source_x) & (index_z == source_z)).astype(
        jnp.float32
    )

    def advance(current, previous, forcing):
        padded = padded_2(current, (("tile", 1),), 4)
        return update(padded, previous, speed, absorb, forcing)

    def forward(carry, amplitude):
        current, previous = carry
        updated = advance(current, previous, amplitude * source)
        return ((updated, current), updated)

    _, snapshots = lax.scan(forward, (forward_state[0, 0], forward_state[0, 1]), wavelet[0])

    def backward(carry, inputs_step):
        current, previous, summed = carry
        snapshot, record = inputs_step
        updated = advance(current, previous, record[:, :, None] * plane)
        return ((updated, current, summed + snapshot * updated), None)

    start_state = (adjoint_state[0, 0], adjoint_state[0, 1], zeros_field)
    (_, _, summed), _ = lax.scan(backward, start_state, (snapshots[::-1], receiver_data[0][::-1]))
    partial_value = summed / steps_count
    wanted = jnp.arange(block_rows * lax.axis_size("shot"), dtype=jnp.int32) - first_row
    valid = ((wanted >= 0) & (wanted < span_y))[:, None, None]
    safe = jnp.clip(wanted, 0, span_y - 1)
    return lax.psum_scatter(
        jnp.where(valid, jnp.take(partial_value, safe, axis=0), 0.0),
        "shot",
        scatter_dimension=0,
        tiled=True,
    )


def solution(mesh):
    placed = (
        P("shot", "tile", None),
        P("shot", "tile", None),
        P(),
        P("shot"),
        P("shot"),
        P("shot", None),
        P("shot", None, None, "tile"),
        P("shot", None, None, "tile", None),
        P("shot", None, None, "tile", None),
    )
    return jax.shard_map(
        body, mesh=mesh, in_specs=placed, out_specs=P("shot", "tile", None), check_vma=False
    )
```

profile of v0, /device:TPU:65, one launch (start us, length us, event | category | flops | bytes accessed | tf_op | source)
XLA Modules:
  0.0 571.7 jit_solution(12189477298314424256)
XLA Ops:
  13.2 3.5 slice_bitcast_fusion
  18.2 48.9 %all-gather.3.cloned.1.call-done = f32[256,32,128]{2,1,0:T(8,128)} async-done(((f32[16,32,128]{2,1,0:T(8,128)}), f32[256,32,128]{2,1,0:T(8,128)}) %all-gather.3.cloned.1.call-update) | async-done | bytes 4194320 | tf_op jit(solution)/shard_map/all_gather | solution.py:79
  67.1 4.1 gather_fusion.1
  71.2 51.5 %all-gather.5.cloned.1.call-done = f32[256,32,128]{2,1,0:T(8,128)} async-done(((f32[16,32,128]{2,1,0:T(8,128)}), f32[256,32,128]{2,1,0:T(8,128)}) %all-gather.5.cloned.1.call-update) | async-done | bytes 4194320 | tf_op jit(solution)/shard_map/all_gather | solution.py:78
  122.6 4.0 gather_fusion.2
  126.6 4.0 select_select_fusion.1
  130.6 161.2 %while.34 = (s32[]{:T(128)}, f32[96,32,128]{2,1,0:T(8,128)S(1)}, f32[96,32,128]{2,1,0:T(8,128)}, f32[8,96,32,128]{3,2,1,0:T(8,128)}, f32[96,32,128]{2,1,0:T(8,12...) while((s32[]{:T(128)}, f32[96,32,128]{2,1,0:T(8,128)S(1)}, ...), condition=%wide.region_1.3_spmd.clone, body=%wide.region_0.2_spmd.clone.sunk | while | flops 17301504 | bytes 40701828 | solution.py:111
  133.5 3.2 collective-permute-start
  139.8 4.1 collective-permute-done
  143.9 7.2 %bitcast_dynamic-update-slice_fusion.2 = (f32[8,96,32,128]{3,2,1,0:T(8,128)}, f32[96,32,128]{2,1,0:T(8,128)S(1)}) fusion(f32[8,96,32,128]{3,2,1,0:T(8,128)} %get-tuple-element.470, s32[]{:T(128)S(6)} %copy.20, f32[96,32,128]{2,1,0:T(8,128)S(1)} %copy-done.1, f32[]{:T(128)} %bitcast.31, pred[128]{0:T(512)(128)(4,1)S(1)} %get-tuple-element.484, ...), kind=kLoop, calls=%fused_computation.63.clone.1 | loop fusion | flops 17301504 | bytes 15928964 | tf_op jit(solution)/shard_map/while/body/jit(dynamic_update_index_in_dim)/dynamic_update_slice | solution.py:111
  155.3 3.2 collective-permute-start
  160.6 4.6 collective-permute-done
  165.2 7.2 %bitcast_dynamic-update-slice_fusion.2 = (f32[8,96,32,128]{3,2,1,0:T(8,128)}, f32[96,32,128]{2,1,0:T(8,128)S(1)}) fusion(f32[8,96,32,128]{3,2,1,0:T(8,128)} %get-tuple-element.470, s32[]{:T(128)S(6)} %copy.20, f32[96,32,128]{2,1,0:T(8,128)S(1)} %copy-done.1, f32[]{:T(128)} %bitcast.31, pred[128]{0:T(512)(128)(4,1)S(1)} %get-tuple-element.484, ...), kind=kLoop, calls=%fused_computation.63.clone.1 | loop fusion | flops 17301504 | bytes 15928964 | tf_op jit(solution)/shard_map/while/body/jit(dynamic_update_index_in_dim)/dynamic_update_slice | solution.py:111
  176.5 3.3 collective-permute-start
  181.6 2.7 collective-permute-done
  184.3 7.2 %bitcast_dynamic-update-slice_fusion.2 = (f32[8,96,32,128]{3,2,1,0:T(8,128)}, f32[96,32,128]{2,1,0:T(8,128)S(1)}) fusion(f32[8,96,32,128]{3,2,1,0:T(8,128)} %get-tuple-element.470, s32[]{:T(128)S(6)} %copy.20, f32[96,32,128]{2,1,0:T(8,128)S(1)} %copy-done.1, f32[]{:T(128)} %bitcast.31, pred[128]{0:T(512)(128)(4,1)S(1)} %get-tuple-element.484, ...), kind=kLoop, calls=%fused_computation.63.clone.1 | loop fusion | flops 17301504 | bytes 15928964 | tf_op jit(solution)/shard_map/while/body/jit(dynamic_update_index_in_dim)/dynamic_update_slice | solution.py:111
  195.5 4.0 collective-permute-start
  201.0 2.7 collective-permute-done
  203.7 7.2 %bitcast_dynamic-update-slice_fusion.2 = (f32[8,96,32,128]{3,2,1,0:T(8,128)}, f32[96,32,128]{2,1,0:T(8,128)S(1)}) fusion(f32[8,96,32,128]{3,2,1,0:T(8,128)} %get-tuple-element.470, s32[]{:T(128)S(6)} %copy.20, f32[96,32,128]{2,1,0:T(8,128)S(1)} %copy-done.1, f32[]{:T(128)} %bitcast.31, pred[128]{0:T(512)(128)(4,1)S(1)} %get-tuple-element.484, ...), kind=kLoop, calls=%fused_computation.63.clone.1 | loop fusion | flops 17301504 | bytes 15928964 | tf_op jit(solution)/shard_map/while/body/jit(dynamic_update_index_in_dim)/dynamic_update_slice | solution.py:111
  213.0 2.1 collective-permute-start.1
  215.1 3.6 collective-permute-start
  220.2 3.4 collective-permute-done
  223.6 7.2 %bitcast_dynamic-update-slice_fusion.2 = (f32[8,96,32,128]{3,2,1,0:T(8,128)}, f32[96,32,128]{2,1,0:T(8,128)S(1)}) fusion(f32[8,96,32,128]{3,2,1,0:T(8,128)} %get-tuple-element.470, s32[]{:T(128)S(6)} %copy.20, f32[96,32,128]{2,1,0:T(8,128)S(1)} %copy-done.1, f32[]{:T(128)} %bitcast.31, pred[128]{0:T(512)(128)(4,1)S(1)} %get-tuple-element.484, ...), kind=kLoop, calls=%fused_computation.63.clone.1 | loop fusion | flops 17301504 | bytes 15928964 | tf_op jit(solution)/shard_map/while/body/jit(dynamic_update_index_in_dim)/dynamic_update_slice | solution.py:111
  235.0 3.6 collective-permute-start
  240.1 3.4 collective-permute-done
  243.5 7.2 %bitcast_dynamic-update-slice_fusion.2 = (f32[8,96,32,128]{3,2,1,0:T(8,128)}, f32[96,32,128]{2,1,0:T(8,128)S(1)}) fusion(f32[8,96,32,128]{3,2,1,0:T(8,128)} %get-tuple-element.470, s32[]{:T(128)S(6)} %copy.20, f32[96,32,128]{2,1,0:T(8,128)S(1)} %copy-done.1, f32[]{:T(128)} %bitcast.31, pred[128]{0:T(512)(128)(4,1)S(1)} %get-tuple-element.484, ...), kind=kLoop, calls=%fused_computation.63.clone.1 | loop fusion | flops 17301504 | bytes 15928964 | tf_op jit(solution)/shard_map/while/body/jit(dynamic_update_index_in_dim)/dynamic_update_slice | solution.py:111
  252.8 2.1 collective-permute-start.1
  254.9 3.6 collective-permute-start
  260.0 3.4 collective-permute-done
  263.4 7.2 %bitcast_dynamic-update-slice_fusion.2 = (f32[8,96,32,128]{3,2,1,0:T(8,128)}, f32[96,32,128]{2,1,0:T(8,128)S(1)}) fusion(f32[8,96,32,128]{3,2,1,0:T(8,128)} %get-tuple-element.470, s32[]{:T(128)S(6)} %copy.20, f32[96,32,128]{2,1,0:T(8,128)S(1)} %copy-done.1, f32[]{:T(128)} %bitcast.31, pred[128]{0:T(512)(128)(4,1)S(1)} %get-tuple-element.484, ...), kind=kLoop, calls=%fused_computation.63.clone.1 | loop fusion | flops 17301504 | bytes 15928964 | tf_op jit(solution)/shard_map/while/body/jit(dynamic_update_index_in_dim)/dynamic_update_slice | solution.py:111
  274.8 3.6 collective-permute-start
  279.9 3.4 collective-permute-done
  283.3 7.2 %bitcast_dynamic-update-slice_fusion.2 = (f32[8,96,32,128]{3,2,1,0:T(8,128)}, f32[96,32,128]{2,1,0:T(8,128)S(1)}) fusion(f32[8,96,32,128]{3,2,1,0:T(8,128)} %get-tuple-element.470, s32[]{:T(128)S(6)} %copy.20, f32[96,32,128]{2,1,0:T(8,128)S(1)} %copy-done.1, f32[]{:T(128)} %bitcast.31, pred[128]{0:T(512)(128)(4,1)S(1)} %get-tuple-element.484, ...), kind=kLoop, calls=%fused_computation.63.clone.1 | loop fusion | flops 17301504 | bytes 15928964 | tf_op jit(solution)/shard_map/while/body/jit(dynamic_update_index_in_dim)/dynamic_update_slice | solution.py:111
  291.8 10.6 %rev.7 = f32[8,96,32,128]{3,2,1,0:T(8,128)} reverse(f32[8,96,32,128]{3,2,1,0:T(8,128)} %get-tuple-element.220), dimensions={0} | reverse | bytes 25165824 | tf_op jit(solution)/shard_map/rev | solution.py:120
  302.4 171.3 %while.35 = (s32[]{:T(128)}, f32[96,32,128]{2,1,0:T(8,128)S(1)}, f32[96,32,128]{2,1,0:T(8,128)}, f32[96,32,128]{2,1,0:T(8,128)}, f32[96,32,128]{2,1,0:T(8,128)},...) while((s32[]{:T(128)}, f32[96,32,128]{2,1,0:T(8,128)S(1)}, ...), condition=%wide.region_3.5_spmd.clone, body=%wide.region_2.4_spmd.clone.sunk | while | flops 18088196 | bytes 31298776 | solution.py:120
  303.3 2.1 collective-permute-start.3
  305.4 3.6 collective-permute-start.2
  311.6 2.4 collective-permute-done.2
  314.0 7.9 %fusion.87 = (f32[96,32,128]{2,1,0:T(8,128)}, f32[96,32,128]{2,1,0:T(8,128)S(1)}) fusion(f32[96,32,128]{2,1,0:T(8,128)} %get-tuple-element.501, f32[8,96,32,128]{3,2,1,0:T(8,128)} %get-tuple-element.516, s32[]{:T(128)S(6)} %copy.32, pred[]{:T(512)S(6)} %compare.8, f32[96,32,128]{2,1,0:T(8,128)} %get-tuple-element.513, f32[128]{0:T(128)S(1)} %fusion.85, ...), kind=kLoop, calls=%fused_computation.125.clone.1 | loop fusion | flops 18087936 | bytes 19083780 | tf_op jit(solution)/shard_map/while/body/eval_jaxpr/add | solution.py:117
  323.9 2.1 collective-permute-start.3
  326.1 3.5 collective-permute-start.2
  332.2 2.7 collective-permute-done.2
  335.0 8.0 %fusion.87 = (f32[96,32,128]{2,1,0:T(8,128)}, f32[96,32,128]{2,1,0:T(8,128)S(1)}) fusion(f32[96,32,128]{2,1,0:T(8,128)} %get-tuple-element.501, f32[8,96,32,128]{3,2,1,0:T(8,128)} %get-tuple-element.516, s32[]{:T(128)S(6)} %copy.32, pred[]{:T(512)S(6)} %compare.8, f32[96,32,128]{2,1,0:T(8,128)} %get-tuple-element.513, f32[128]{0:T(128)S(1)} %fusion.85, ...), kind=kLoop, calls=%fused_computation.125.clone.1 | loop fusion | flops 18087936 | bytes 19083780 | tf_op jit(solution)/shard_map/while/body/eval_jaxpr/add | solution.py:117
  347.2 3.6 collective-permute-start.2
  353.3 3.5 collective-permute-done.2
  356.8 8.0 %fusion.87 = (f32[96,32,128]{2,1,0:T(8,128)}, f32[96,32,128]{2,1,0:T(8,128)S(1)}) fusion(f32[96,32,128]{2,1,0:T(8,128)} %get-tuple-element.501, f32[8,96,32,128]{3,2,1,0:T(8,128)} %get-tuple-element.516, s32[]{:T(128)S(6)} %copy.32, pred[]{:T(512)S(6)} %compare.8, f32[96,32,128]{2,1,0:T(8,128)} %get-tuple-element.513, f32[128]{0:T(128)S(1)} %fusion.85, ...), kind=kLoop, calls=%fused_computation.125.clone.1 | loop fusion | flops 18087936 | bytes 19083780 | tf_op jit(solution)/shard_map/while/body/eval_jaxpr/add | solution.py:117
  368.8 3.4 collective-permute-start.2
  374.8 3.1 collective-permute-done.2
  378.0 8.0 %fusion.87 = (f32[96,32,128]{2,1,0:T(8,128)}, f32[96,32,128]{2,1,0:T(8,128)S(1)}) fusion(f32[96,32,128]{2,1,0:T(8,128)} %get-tuple-element.501, f32[8,96,32,128]{3,2,1,0:T(8,128)} %get-tuple-element.516, s32[]{:T(128)S(6)} %copy.32, pred[]{:T(512)S(6)} %compare.8, f32[96,32,128]{2,1,0:T(8,128)} %get-tuple-element.513, f32[128]{0:T(128)S(1)} %fusion.85, ...), kind=kLoop, calls=%fused_computation.125.clone.1 | loop fusion | flops 18087936 | bytes 19083780 | tf_op jit(solution)/shard_map/while/body/eval_jaxpr/add | solution.py:117
  390.0 3.9 collective-permute-start.2
  396.5 2.9 collective-permute-done.2
  399.4 8.0 %fusion.87 = (f32[96,32,128]{2,1,0:T(8,128)}, f32[96,32,128]{2,1,0:T(8,128)S(1)}) fusion(f32[96,32,128]{2,1,0:T(8,128)} %get-tuple-element.501, f32[8,96,32,128]{3,2,1,0:T(8,128)} %get-tuple-element.516, s32[]{:T(128)S(6)} %copy.32, pred[]{:T(512)S(6)} %compare.8, f32[96,32,128]{2,1,0:T(8,128)} %get-tuple-element.513, f32[128]{0:T(128)S(1)} %fusion.85, ...), kind=kLoop, calls=%fused_computation.125.clone.1 | loop fusion | flops 18087936 | bytes 19083780 | tf_op jit(solution)/shard_map/while/body/eval_jaxpr/add | solution.py:117
  411.4 4.0 collective-permute-start.2
  418.0 3.0 collective-permute-done.2
  421.1 8.1 %fusion.87 = (f32[96,32,128]{2,1,0:T(8,128)}, f32[96,32,128]{2,1,0:T(8,128)S(1)}) fusion(f32[96,32,128]{2,1,0:T(8,128)} %get-tuple-element.501, f32[8,96,32,128]{3,2,1,0:T(8,128)} %get-tuple-element.516, s32[]{:T(128)S(6)} %copy.32, pred[]{:T(512)S(6)} %compare.8, f32[96,32,128]{2,1,0:T(8,128)} %get-tuple-element.513, f32[128]{0:T(128)S(1)} %fusion.85, ...), kind=kLoop, calls=%fused_computation.125.clone.1 | loop fusion | flops 18087936 | bytes 19083780 | tf_op jit(solution)/shard_map/while/body/eval_jaxpr/add | solution.py:117
  433.2 4.0 collective-permute-start.2
  439.8 2.9 collective-permute-done.2
  442.7 8.1 %fusion.87 = (f32[96,32,128]{2,1,0:T(8,128)}, f32[96,32,128]{2,1,0:T(8,128)S(1)}) fusion(f32[96,32,128]{2,1,0:T(8,128)} %get-tuple-element.501, f32[8,96,32,128]{3,2,1,0:T(8,128)} %get-tuple-element.516, s32[]{:T(128)S(6)} %copy.32, pred[]{:T(512)S(6)} %compare.8, f32[96,32,128]{2,1,0:T(8,128)} %get-tuple-element.513, f32[128]{0:T(128)S(1)} %fusion.85, ...), kind=kLoop, calls=%fused_computation.125.clone.1 | loop fusion | flops 18087936 | bytes 19083780 | tf_op jit(solution)/shard_map/while/body/eval_jaxpr/add | solution.py:117
  454.8 4.0 collective-permute-start.2
  461.4 3.0 collective-permute-done.2
  464.5 8.0 %fusion.87 = (f32[96,32,128]{2,1,0:T(8,128)}, f32[96,32,128]{2,1,0:T(8,128)S(1)}) fusion(f32[96,32,128]{2,1,0:T(8,128)} %get-tuple-element.501, f32[8,96,32,128]{3,2,1,0:T(8,128)} %get-tuple-element.516, s32[]{:T(128)S(6)} %copy.32, pred[]{:T(512)S(6)} %compare.8, f32[96,32,128]{2,1,0:T(8,128)} %get-tuple-element.513, f32[128]{0:T(128)S(1)} %fusion.85, ...), kind=kLoop, calls=%fused_computation.125.clone.1 | loop fusion | flops 18087936 | bytes 19083780 | tf_op jit(solution)/shard_map/while/body/eval_jaxpr/add | solution.py:117
  475.3 3.1 gather_fusion
  478.5 4.5 select_select_fusion
  483.0 82.2 %reduce-scatter.2.cloned.1.call-done = f32[16,32,128]{2,1,0:T(8,128)} async-done(((f32[256,32,128]{2,1,0:T(8,128)}), f32[16,32,128]{2,1,0:T(8,128)}) %reduce-scatter.2.cloned.1.call-update) | async-done | bytes 262160 | tf_op jit(solution)/shard_map/reduce_scatter | solution.py:125
  (195 shorter events, 100.4 us)
Async XLA Ops:
  6.5 4.1 copy-start.5
  6.5 60.6 %all-gather.3.cloned.1.call-start = ((), (), s32[]{:S(2)}) async-start(), calls=%async_computation.1 | async-start | bytes 4456448 | tf_op jit(solution)/shard_map/all_gather | solution.py:79
  7.3 115.4 %all-gather.5.cloned.1.call-start = ((), (), s32[]{:S(2)}) async-start(), calls=%async_computation.2 | async-start | bytes 4456448 | tf_op jit(solution)/shard_map/all_gather | solution.py:78
  8.0 557.2 %reduce-scatter.2.cloned.1.call-start = ((), (), s32[]{:S(2)}) async-start(), calls=%async_computation.3 | async-start | bytes 4456448 | tf_op jit(solution)/shard_map/reduce_scatter | solution.py:125
  13.2 3.6 copy-start.2
  131.4 8.3 %collective-permute-start.1 = (f32[96,4,128]{2,1,0:T(4,128)}, f32[96,4,128]{2,1,0:T(4,128)S(1)}, u32[]{:S(2)}, u32[]{:S(2)}) collective-permute-start(f32[96,4,128]{2,1,0:T(4,128)} %get-tuple-element.441), channel_id=1, source_target_pairs={{1,0},{2,1},{3,2},{4,3},{5,4},{6,5},{7,6},{9,8},{10,9},{11,10},{12... | collective-permute-start | bytes 589832 | tf_op jit(solution)/shard_map/while/body/eval_jaxpr/ppermute | solution.py:19
  133.5 10.4 %collective-permute-start = (f32[96,4,128]{2,1,0:T(4,128)}, f32[96,4,128]{2,1,0:T(4,128)S(1)}, u32[]{:S(2)}, u32[]{:S(2)}) collective-permute-start(f32[96,4,128]{2,1,0:T(4,128)} %get-tuple-element.440), channel_id=1, source_target_pairs={{0,1},{1,2},{2,3},{3,4},{4,5},{5,6},{6,7},{8,9},{9,10},{10,11},{11... | collective-permute-start | bytes 589832 | tf_op jit(solution)/shard_map/while/body/eval_jaxpr/ppermute | solution.py:17
  137.9 5.9 %copy-start = (f32[96,32,128]{2,1,0:T(8,128)S(1)}, f32[96,32,128]{2,1,0:T(8,128)}, u32[]{:S(2)}) copy-start(f32[96,32,128]{2,1,0:T(8,128)} %get-tuple-element.482) | copy-start | bytes 4718596 | tf_op jit(solution)/shard_map/while
  137.9 5.9 %copy-start.1 = (f32[96,32,128]{2,1,0:T(8,128)S(1)}, f32[96,32,128]{2,1,0:T(8,128)}, u32[]{:S(2)}) copy-start(f32[96,32,128]{2,1,0:T(8,128)} %get-tuple-element.481) | copy-start | bytes 4718596 | tf_op jit(solution)/shard_map/while
  153.2 7.4 %collective-permute-start.1 = (f32[96,4,128]{2,1,0:T(4,128)}, f32[96,4,128]{2,1,0:T(4,128)S(1)}, u32[]{:S(2)}, u32[]{:S(2)}) collective-permute-start(f32[96,4,128]{2,1,0:T(4,128)} %get-tuple-element.441), channel_id=1, source_target_pairs={{1,0},{2,1},{3,2},{4,3},{5,4},{6,5},{7,6},{9,8},{10,9},{11,10},{12... | collective-permute-start | bytes 589832 | tf_op jit(solution)/shard_map/while/body/eval_jaxpr/ppermute | solution.py:19
  155.3 10.0 %collective-permute-start = (f32[96,4,128]{2,1,0:T(4,128)}, f32[96,4,128]{2,1,0:T(4,128)S(1)}, u32[]{:S(2)}, u32[]{:S(2)}) collective-permute-start(f32[96,4,128]{2,1,0:T(4,128)} %get-tuple-element.440), channel_id=1, source_target_pairs={{0,1},{1,2},{2,3},{3,4},{4,5},{5,6},{6,7},{8,9},{9,10},{10,11},{11... | collective-permute-start | bytes 589832 | tf_op jit(solution)/shard_map/while/body/eval_jaxpr/ppermute | solution.py:17
  159.7 5.6 copy-start
  159.7 5.6 copy-start.1
  174.6 7.0 %collective-permute-start.1 = (f32[96,4,128]{2,1,0:T(4,128)}, f32[96,4,128]{2,1,0:T(4,128)S(1)}, u32[]{:S(2)}, u32[]{:S(2)}) collective-permute-start(f32[96,4,128]{2,1,0:T(4,128)} %get-tuple-element.441), channel_id=1, source_target_pairs={{1,0},{2,1},{3,2},{4,3},{5,4},{6,5},{7,6},{9,8},{10,9},{11,10},{12... | collective-permute-start | bytes 589832 | tf_op jit(solution)/shard_map/while/body/eval_jaxpr/ppermute | solution.py:19
  176.5 7.8 %collective-permute-start = (f32[96,4,128]{2,1,0:T(4,128)}, f32[96,4,128]{2,1,0:T(4,128)S(1)}, u32[]{:S(2)}, u32[]{:S(2)}) collective-permute-start(f32[96,4,128]{2,1,0:T(4,128)} %get-tuple-element.440), channel_id=1, source_target_pairs={{0,1},{1,2},{2,3},{3,4},{4,5},{5,6},{6,7},{8,9},{9,10},{10,11},{11... | collective-permute-start | bytes 589832 | tf_op jit(solution)/shard_map/while/body/eval_jaxpr/ppermute | solution.py:17
  181.1 3.2 copy-start
  181.1 3.2 copy-start.1
  193.6 7.3 %collective-permute-start.1 = (f32[96,4,128]{2,1,0:T(4,128)}, f32[96,4,128]{2,1,0:T(4,128)S(1)}, u32[]{:S(2)}, u32[]{:S(2)}) collective-permute-start(f32[96,4,128]{2,1,0:T(4,128)} %get-tuple-element.441), channel_id=1, source_target_pairs={{1,0},{2,1},{3,2},{4,3},{5,4},{6,5},{7,6},{9,8},{10,9},{11,10},{12... | collective-permute-start | bytes 589832 | tf_op jit(solution)/shard_map/while/body/eval_jaxpr/ppermute | solution.py:19
  195.5 8.1 %collective-permute-start = (f32[96,4,128]{2,1,0:T(4,128)}, f32[96,4,128]{2,1,0:T(4,128)S(1)}, u32[]{:S(2)}, u32[]{:S(2)}) collective-permute-start(f32[96,4,128]{2,1,0:T(4,128)} %get-tuple-element.440), channel_id=1, source_target_pairs={{0,1},{1,2},{2,3},{3,4},{4,5},{5,6},{6,7},{8,9},{9,10},{10,11},{11... | collective-permute-start | bytes 589832 | tf_op jit(solution)/shard_map/while/body/eval_jaxpr/ppermute | solution.py:17
  200.8 2.9 copy-start
  200.8 2.9 copy-start.1
  213.0 7.1 %collective-permute-start.1 = (f32[96,4,128]{2,1,0:T(4,128)}, f32[96,4,128]{2,1,0:T(4,128)S(1)}, u32[]{:S(2)}, u32[]{:S(2)}) collective-permute-start(f32[96,4,128]{2,1,0:T(4,128)} %get-tuple-element.441), channel_id=1, source_target_pairs={{1,0},{2,1},{3,2},{4,3},{5,4},{6,5},{7,6},{9,8},{10,9},{11,10},{12... | collective-permute-start | bytes 589832 | tf_op jit(solution)/shard_map/while/body/eval_jaxpr/ppermute | solution.py:19
  215.1 8.4 %collective-permute-start = (f32[96,4,128]{2,1,0:T(4,128)}, f32[96,4,128]{2,1,0:T(4,128)S(1)}, u32[]{:S(2)}, u32[]{:S(2)}) collective-permute-start(f32[96,4,128]{2,1,0:T(4,128)} %get-tuple-element.440), channel_id=1, source_target_pairs={{0,1},{1,2},{2,3},{3,4},{4,5},{5,6},{6,7},{8,9},{9,10},{10,11},{11... | collective-permute-start | bytes 589832 | tf_op jit(solution)/shard_map/while/body/eval_jaxpr/ppermute | solution.py:17
  220.0 3.6 copy-start
  220.0 3.6 copy-start.1
  232.9 7.1 %collective-permute-start.1 = (f32[96,4,128]{2,1,0:T(4,128)}, f32[96,4,128]{2,1,0:T(4,128)S(1)}, u32[]{:S(2)}, u32[]{:S(2)}) collective-permute-start(f32[96,4,128]{2,1,0:T(4,128)} %get-tuple-element.441), channel_id=1, source_target_pairs={{1,0},{2,1},{3,2},{4,3},{5,4},{6,5},{7,6},{9,8},{10,9},{11,10},{12... | collective-permute-start | bytes 589832 | tf_op jit(solution)/shard_map/while/body/eval_jaxpr/ppermute | solution.py:19
  235.0 8.4 %collective-permute-start = (f32[96,4,128]{2,1,0:T(4,128)}, f32[96,4,128]{2,1,0:T(4,128)S(1)}, u32[]{:S(2)}, u32[]{:S(2)}) collective-permute-start(f32[96,4,128]{2,1,0:T(4,128)} %get-tuple-element.440), channel_id=1, source_target_pairs={{0,1},{1,2},{2,3},{3,4},{4,5},{5,6},{6,7},{8,9},{9,10},{10,11},{11... | collective-permute-start | bytes 589832 | tf_op jit(solution)/shard_map/while/body/eval_jaxpr/ppermute | solution.py:17
  239.9 3.6 copy-start
  239.9 3.6 copy-start.1
  252.8 7.1 %collective-permute-start.1 = (f32[96,4,128]{2,1,0:T(4,128)}, f32[96,4,128]{2,1,0:T(4,128)S(1)}, u32[]{:S(2)}, u32[]{:S(2)}) collective-permute-start(f32[96,4,128]{2,1,0:T(4,128)} %get-tuple-element.441), channel_id=1, source_target_pairs={{1,0},{2,1},{3,2},{4,3},{5,4},{6,5},{7,6},{9,8},{10,9},{11,10},{12... | collective-permute-start | bytes 589832 | tf_op jit(solution)/shard_map/while/body/eval_jaxpr/ppermute | solution.py:19
  254.9 8.4 %collective-permute-start = (f32[96,4,128]{2,1,0:T(4,128)}, f32[96,4,128]{2,1,0:T(4,128)S(1)}, u32[]{:S(2)}, u32[]{:S(2)}) collective-permute-start(f32[96,4,128]{2,1,0:T(4,128)} %get-tuple-element.440), channel_id=1, source_target_pairs={{0,1},{1,2},{2,3},{3,4},{4,5},{5,6},{6,7},{8,9},{9,10},{10,11},{11... | collective-permute-start | bytes 589832 | tf_op jit(solution)/shard_map/while/body/eval_jaxpr/ppermute | solution.py:17
  259.8 3.6 copy-start
  259.8 3.6 copy-start.1
  272.7 7.1 %collective-permute-start.1 = (f32[96,4,128]{2,1,0:T(4,128)}, f32[96,4,128]{2,1,0:T(4,128)S(1)}, u32[]{:S(2)}, u32[]{:S(2)}) collective-permute-start(f32[96,4,128]{2,1,0:T(4,128)} %get-tuple-element.441), channel_id=1, source_target_pairs={{1,0},{2,1},{3,2},{4,3},{5,4},{6,5},{7,6},{9,8},{10,9},{11,10},{12... | collective-permute-start | bytes 589832 | tf_op jit(solution)/shard_map/while/body/eval_jaxpr/ppermute | solution.py:19
  274.8 8.4 %collective-permute-start = (f32[96,4,128]{2,1,0:T(4,128)}, f32[96,4,128]{2,1,0:T(4,128)S(1)}, u32[]{:S(2)}, u32[]{:S(2)}) collective-permute-start(f32[96,4,128]{2,1,0:T(4,128)} %get-tuple-element.440), channel_id=1, source_target_pairs={{0,1},{1,2},{2,3},{3,4},{4,5},{5,6},{6,7},{8,9},{9,10},{10,11},{11... | collective-permute-start | bytes 589832 | tf_op jit(solution)/shard_map/while/body/eval_jaxpr/ppermute | solution.py:17
  279.7 3.6 copy-start
  279.7 3.6 copy-start.1
  303.3 7.3 %collective-permute-start.3 = (f32[96,4,128]{2,1,0:T(4,128)}, f32[96,4,128]{2,1,0:T(4,128)}, u32[]{:S(2)}, u32[]{:S(2)}) collective-permute-start(f32[96,4,128]{2,1,0:T(4,128)} %get-tuple-element.454), channel_id=1, source_target_pairs={{1,0},{2,1},{3,2},{4,3},{5,4},{6,5},{7,6},{9,8},{10,9},{11,10},{12... | collective-permute-start | bytes 589832 | tf_op jit(solution)/shard_map/while/body/eval_jaxpr/ppermute | solution.py:19
  305.4 8.5 %collective-permute-start.2 = (f32[96,4,128]{2,1,0:T(4,128)}, f32[96,4,128]{2,1,0:T(4,128)}, u32[]{:S(2)}, u32[]{:S(2)}) collective-permute-start(f32[96,4,128]{2,1,0:T(4,128)} %get-tuple-element.453), channel_id=1, source_target_pairs={{0,1},{1,2},{2,3},{3,4},{4,5},{5,6},{6,7},{8,9},{9,10},{10,11},{11... | collective-permute-start | bytes 589832 | tf_op jit(solution)/shard_map/while/body/eval_jaxpr/ppermute | solution.py:17
  323.9 7.3 %collective-permute-start.3 = (f32[96,4,128]{2,1,0:T(4,128)}, f32[96,4,128]{2,1,0:T(4,128)}, u32[]{:S(2)}, u32[]{:S(2)}) collective-permute-start(f32[96,4,128]{2,1,0:T(4,128)} %get-tuple-element.454), channel_id=1, source_target_pairs={{1,0},{2,1},{3,2},{4,3},{5,4},{6,5},{7,6},{9,8},{10,9},{11,10},{12... | collective-permute-start | bytes 589832 | tf_op jit(solution)/shard_map/while/body/eval_jaxpr/ppermute | solution.py:19
  326.1 8.9 %collective-permute-start.2 = (f32[96,4,128]{2,1,0:T(4,128)}, f32[96,4,128]{2,1,0:T(4,128)}, u32[]{:S(2)}, u32[]{:S(2)}) collective-permute-start(f32[96,4,128]{2,1,0:T(4,128)} %get-tuple-element.453), channel_id=1, source_target_pairs={{0,1},{1,2},{2,3},{3,4},{4,5},{5,6},{6,7},{8,9},{9,10},{10,11},{11... | collective-permute-start | bytes 589832 | tf_op jit(solution)/shard_map/while/body/eval_jaxpr/ppermute | solution.py:17
  345.1 7.2 %collective-permute-start.3 = (f32[96,4,128]{2,1,0:T(4,128)}, f32[96,4,128]{2,1,0:T(4,128)}, u32[]{:S(2)}, u32[]{:S(2)}) collective-permute-start(f32[96,4,128]{2,1,0:T(4,128)} %get-tuple-element.454), channel_id=1, source_target_pairs={{1,0},{2,1},{3,2},{4,3},{5,4},{6,5},{7,6},{9,8},{10,9},{11,10},{12... | collective-permute-start | bytes 589832 | tf_op jit(solution)/shard_map/while/body/eval_jaxpr/ppermute | solution.py:19
  347.2 9.7 %collective-permute-start.2 = (f32[96,4,128]{2,1,0:T(4,128)}, f32[96,4,128]{2,1,0:T(4,128)}, u32[]{:S(2)}, u32[]{:S(2)}) collective-permute-start(f32[96,4,128]{2,1,0:T(4,128)} %get-tuple-element.453), channel_id=1, source_target_pairs={{0,1},{1,2},{2,3},{3,4},{4,5},{5,6},{6,7},{8,9},{9,10},{10,11},{11... | collective-permute-start | bytes 589832 | tf_op jit(solution)/shard_map/while/body/eval_jaxpr/ppermute | solution.py:17
  366.9 6.9 %collective-permute-start.3 = (f32[96,4,128]{2,1,0:T(4,128)}, f32[96,4,128]{2,1,0:T(4,128)}, u32[]{:S(2)}, u32[]{:S(2)}) collective-permute-start(f32[96,4,128]{2,1,0:T(4,128)} %get-tuple-element.454), channel_id=1, source_target_pairs={{1,0},{2,1},{3,2},{4,3},{5,4},{6,5},{7,6},{9,8},{10,9},{11,10},{12... | collective-permute-start | bytes 589832 | tf_op jit(solution)/shard_map/while/body/eval_jaxpr/ppermute | solution.py:19
  368.8 9.2 %collective-permute-start.2 = (f32[96,4,128]{2,1,0:T(4,128)}, f32[96,4,128]{2,1,0:T(4,128)}, u32[]{:S(2)}, u32[]{:S(2)}) collective-permute-start(f32[96,4,128]{2,1,0:T(4,128)} %get-tuple-element.453), channel_id=1, source_target_pairs={{0,1},{1,2},{2,3},{3,4},{4,5},{5,6},{6,7},{8,9},{9,10},{10,11},{11... | collective-permute-start | bytes 589832 | tf_op jit(solution)/shard_map/while/body/eval_jaxpr/ppermute | solution.py:17
  388.1 7.4 %collective-permute-start.3 = (f32[96,4,128]{2,1,0:T(4,128)}, f32[96,4,128]{2,1,0:T(4,128)}, u32[]{:S(2)}, u32[]{:S(2)}) collective-permute-start(f32[96,4,128]{2,1,0:T(4,128)} %get-tuple-element.454), channel_id=1, source_target_pairs={{1,0},{2,1},{3,2},{4,3},{5,4},{6,5},{7,6},{9,8},{10,9},{11,10},{12... | collective-permute-start | bytes 589832 | tf_op jit(solution)/shard_map/while/body/eval_jaxpr/ppermute | solution.py:19
  390.0 9.4 %collective-permute-start.2 = (f32[96,4,128]{2,1,0:T(4,128)}, f32[96,4,128]{2,1,0:T(4,128)}, u32[]{:S(2)}, u32[]{:S(2)}) collective-permute-start(f32[96,4,128]{2,1,0:T(4,128)} %get-tuple-element.453), channel_id=1, source_target_pairs={{0,1},{1,2},{2,3},{3,4},{4,5},{5,6},{6,7},{8,9},{9,10},{10,11},{11... | collective-permute-start | bytes 589832 | tf_op jit(solution)/shard_map/while/body/eval_jaxpr/ppermute | solution.py:17
  409.5 7.5 %collective-permute-start.3 = (f32[96,4,128]{2,1,0:T(4,128)}, f32[96,4,128]{2,1,0:T(4,128)}, u32[]{:S(2)}, u32[]{:S(2)}) collective-permute-start(f32[96,4,128]{2,1,0:T(4,128)} %get-tuple-element.454), channel_id=1, source_target_pairs={{1,0},{2,1},{3,2},{4,3},{5,4},{6,5},{7,6},{9,8},{10,9},{11,10},{12... | collective-permute-start | bytes 589832 | tf_op jit(solution)/shard_map/while/body/eval_jaxpr/ppermute | solution.py:19
  411.4 9.7 %collective-permute-start.2 = (f32[96,4,128]{2,1,0:T(4,128)}, f32[96,4,128]{2,1,0:T(4,128)}, u32[]{:S(2)}, u32[]{:S(2)}) collective-permute-start(f32[96,4,128]{2,1,0:T(4,128)} %get-tuple-element.453), channel_id=1, source_target_pairs={{0,1},{1,2},{2,3},{3,4},{4,5},{5,6},{6,7},{8,9},{9,10},{10,11},{11... | collective-permute-start | bytes 589832 | tf_op jit(solution)/shard_map/while/body/eval_jaxpr/ppermute | solution.py:17
  431.3 7.5 %collective-permute-start.3 = (f32[96,4,128]{2,1,0:T(4,128)}, f32[96,4,128]{2,1,0:T(4,128)}, u32[]{:S(2)}, u32[]{:S(2)}) collective-permute-start(f32[96,4,128]{2,1,0:T(4,128)} %get-tuple-element.454), channel_id=1, source_target_pairs={{1,0},{2,1},{3,2},{4,3},{5,4},{6,5},{7,6},{9,8},{10,9},{11,10},{12... | collective-permute-start | bytes 589832 | tf_op jit(solution)/shard_map/while/body/eval_jaxpr/ppermute | solution.py:19
  433.2 9.5 %collective-permute-start.2 = (f32[96,4,128]{2,1,0:T(4,128)}, f32[96,4,128]{2,1,0:T(4,128)}, u32[]{:S(2)}, u32[]{:S(2)}) collective-permute-start(f32[96,4,128]{2,1,0:T(4,128)} %get-tuple-element.453), channel_id=1, source_target_pairs={{0,1},{1,2},{2,3},{3,4},{4,5},{5,6},{6,7},{8,9},{9,10},{10,11},{11... | collective-permute-start | bytes 589832 | tf_op jit(solution)/shard_map/while/body/eval_jaxpr/ppermute | solution.py:17
  452.9 7.5 %collective-permute-start.3 = (f32[96,4,128]{2,1,0:T(4,128)}, f32[96,4,128]{2,1,0:T(4,128)}, u32[]{:S(2)}, u32[]{:S(2)}) collective-permute-start(f32[96,4,128]{2,1,0:T(4,128)} %get-tuple-element.454), channel_id=1, source_target_pairs={{1,0},{2,1},{3,2},{4,3},{5,4},{6,5},{7,6},{9,8},{10,9},{11,10},{12... | collective-permute-start | bytes 589832 | tf_op jit(solution)/shard_map/while/body/eval_jaxpr/ppermute | solution.py:19
  454.8 9.7 %collective-permute-start.2 = (f32[96,4,128]{2,1,0:T(4,128)}, f32[96,4,128]{2,1,0:T(4,128)}, u32[]{:S(2)}, u32[]{:S(2)}) collective-permute-start(f32[96,4,128]{2,1,0:T(4,128)} %get-tuple-element.453), channel_id=1, source_target_pairs={{0,1},{1,2},{2,3},{3,4},{4,5},{5,6},{6,7},{8,9},{9,10},{10,11},{11... | collective-permute-start | bytes 589832 | tf_op jit(solution)/shard_map/while/body/eval_jaxpr/ppermute | solution.py:17
  475.3 3.2 copy-start.3
  475.3 3.1 copy-start.4
Sparse Core Ops, SparseCore 0:
  9.8 57.2 all-gather.2
  69.6 53.0 all-gather.4
  483.1 81.9 reduce-scatter.1
where the time goes:
time: 577 us; the launch traced here: 572 us
  waiting for transfers between devices  238 us (41%)
  other arithmetic  138 us (24%)
  starting transfers between devices  90.7 us (16%)
  local copies, waits for them, and re-layouts  89.5 us (16%)
  between operations  14.6 us (3%)
    reduce_scatter x1, waiting for transfers between devices, body(): lax.psum_scatter(jnp.where(valid, jnp.take(partial_value, safe, axis=0),...  82.2 us
    add x8, other arithmetic, backward(): return ((updated, current, summed + snapshot * updated), None)  64 us
    ppermute x16, starting transfers between devices, padded_2(): lax.ppermute(tail, axis, [(i, (i + 1) % count) for i in range(ends)])  58.1 us
    dynamic_update_slice x8, other arithmetic, body(): lax.scan(forward, (forward_state[0, 0], forward_state[0, 1]), wavelet[0])  57.4 us
    all_gather x1, waiting for transfers between devices, body(): lax.all_gather(courant, 'shot', axis=0, tiled=True)  51.5 us
    ppermute x16, waiting for transfers between devices, padded_2(): lax.ppermute(tail, axis, [(i, (i + 1) % count) for i in range(ends)])  51.3 us
    all_gather x1, waiting for transfers between devices, body(): lax.all_gather(damping, 'shot', axis=0, tiled=True)  48.9 us
    ppermute x16, starting transfers between devices, padded_2(): lax.ppermute(head, axis, [((i + 1) % count, i) for i in range(ends)])  32.4 us
  transfers between devices with their start and end apart: 35, of which 22 were waited for; matrix products, arithmetic and copies ran while one was open for 8% of the time, Pallas kernels for 0%

commit v1 on v0

v1 whole, which is shorter than its diff:
```python
import functools
import jax
import jax.numpy as jnp
import numpy as np
from jax import lax
from jax.experimental import pallas as pl
from jax.experimental.pallas import tpu as pltpu
from jax.sharding import PartitionSpec as P

MESH_ID = pl.DeviceIdType.MESH
SCALE = 5040.0
WEIGHTS = (-43050.0, 8064.0, -1008.0, 128.0, -9.0)
CENTRES = (-43008.0, -42.0)
NY, NX, NZ = 96, 32, 128
PY = 104
PX = 104


def band_matrix(size, centre):
    band = centre * np.eye(size, dtype=np.float32)
    for offset in range(1, 5):
        band += WEIGHTS[offset] * (np.eye(size, k=offset) + np.eye(size, k=-offset))
    return band


def band_pair():
    deep, wide = band_matrix(NZ, CENTRES[0]), band_matrix(NY, CENTRES[1])
    return (jnp.asarray(np.concatenate([deep, deep], axis=0), jnp.bfloat16),
            jnp.asarray(np.concatenate([wide, wide], axis=1), jnp.bfloat16))


def step_kernel(fwd, adj, extra, speed, absorb, band_z, band_y, out, F, Z, A, C, E, T, image, ssem, rsem):
    s = lax.axis_index("shot")
    t = lax.axis_index("tile")
    core = s % 2
    place = 2 * (t // 2) + core
    left = (s + 1 - 2 * core, t - 2 * (1 - core))
    right = (s + 1 - 2 * core, t + 2 * core)
    has_left = place > 0
    has_right = place < 7

    def halo(f, slot, par, side):
        if side == 0:
            return pltpu.make_async_remote_copy(
                src_ref=F.at[f, slot, pl.ds(4, 4), pl.ds(0, NY), :],
                dst_ref=F.at[f, slot, pl.ds(36, 4), pl.ds(0, NY), :],
                send_sem=ssem.at[f, 0, par], recv_sem=rsem.at[f, 0, par],
                device_id=left, device_id_type=MESH_ID)
        return pltpu.make_async_remote_copy(
            src_ref=F.at[f, slot, pl.ds(32, 4), pl.ds(0, NY), :],
            dst_ref=F.at[f, slot, pl.ds(0, 4), pl.ds(0, NY), :],
            send_sem=ssem.at[f, 1, par], recv_sem=rsem.at[f, 1, par],
            device_id=right, device_id_type=MESH_ID)

    def send(f, slot, par, side):
        @pl.when(has_left if side == 0 else has_right)
        def _():
            halo(f, slot, par, side).start()

    def wait(f, slot, par):
        @pl.when(has_left)
        def _():
            halo(f, slot, par, 0).wait_send()
            halo(f, slot, par, 1).wait_recv()

        @pl.when(has_right)
        def _():
            halo(f, slot, par, 1).wait_send()
            halo(f, slot, par, 0).wait_recv()

    barrier = pltpu.get_barrier_semaphore()

    @pl.when(has_left)
    def _():
        pl.semaphore_signal(barrier, inc=1, device_id=left, device_id_type=MESH_ID)

    @pl.when(has_right)
    def _():
        pl.semaphore_signal(barrier, inc=1, device_id=right, device_id_type=MESH_ID)

    zero_side = jnp.zeros((4, NY, NZ), jnp.float32)
    for f in range(2):
        def clear(slot, carry):
            @pl.when(place == 0)
            def _():
                F[f, slot, pl.ds(0, 4), pl.ds(0, NY), :] = zero_side

            @pl.when(place == 7)
            def _():
                F[f, slot, pl.ds(36, 4), pl.ds(0, NY), :] = zero_side
            return carry
        lax.fori_loop(0, 6, clear, 0)

    def load_states(j, carry):
        rows = pl.ds(pl.multiple_of(8 * j, 8), 8)
        for x in range(NX):
            picked = pl.ds(8 * NX * j + x, 8, stride=NX)
            for f, source in ((0, fwd), (1, adj)):
                F[f, 1, 4 + x, rows, :] = source[0, picked, :]
                F[f, 0, 4 + x, rows, :] = source[1, picked, :]
        return carry

    lax.fori_loop(0, NY // 8, load_states, 0)

    pl.semaphore_wait(barrier, has_left.astype(jnp.int32) + has_right.astype(jnp.int32))

    for f in range(2):
        send(f, 1, 0, 0)
        send(f, 1, 0, 1)

    lane = lax.broadcasted_iota(jnp.int32, (8, NZ), 1)
    row = lax.broadcasted_iota(jnp.int32, (8, NZ), 0)
    depth = jnp.broadcast_to(extra[0, pl.ds(0, 8), pl.ds(34, 1)], (8, NZ))
    plane = jnp.where(lane.astype(jnp.float32) == depth, 0.5, 0.0)
    cell = jnp.broadcast_to(extra[0, pl.ds(0, 8), pl.ds(33, 1)], (8, NZ))

    turns = [(depth + m) - jnp.where(depth + m >= NZ, float(NZ), 0.0) for m in range(8)]

    def load_model(j, carry):
        rows = pl.ds(pl.multiple_of(8 * j, 8), 8)
        for x in range(NX):
            picked = pl.ds(8 * NX * j + x, 8, stride=NX)
            placed = jnp.zeros((8, NZ), jnp.float32)
            for m in range(8):
                value = jnp.broadcast_to(extra[m, rows, pl.ds(x, 1)], (8, NZ))
                placed = jnp.where(lane.astype(jnp.float32) == turns[m], value, placed)
            T[x, rows, :] = placed
            A[x, rows, :] = 2.0 / (1.0 + absorb[picked, :])
            C[x, rows, :] = speed[picked, :] * (0.5 / SCALE)
            index = (place * NX + x) * (NY * NZ) + (row + 8 * j) * NZ + lane
            E[x, rows, :] = jnp.where(index.astype(jnp.float32) == cell, 0.5, 0.0)
            image[x, rows, :] = jnp.zeros((8, NZ), jnp.float32)
        return carry

    lax.fori_loop(0, NY // 8, load_model, 0)

    def across(f, slot, x):
        u = F[f, slot, pl.ds(4 + x, 2), pl.ds(0, NY), :]
        high = u.astype(jnp.bfloat16)
        low = (u - high.astype(jnp.float32)).astype(jnp.bfloat16)
        rows = jnp.concatenate([high.reshape(2 * NY, NZ), low.reshape(2 * NY, NZ)], axis=1)
        deep = jnp.dot(rows, band_z[...], preferred_element_type=jnp.float32)
        sides = jnp.concatenate([jnp.concatenate([high[0], high[1]], axis=1),
                                 jnp.concatenate([low[0], low[1]], axis=1)], axis=0)
        wide = jnp.dot(band_y[...], sides, preferred_element_type=jnp.float32)
        Z[f, x, pl.ds(0, NY), :] = deep[:NY] + wide[:, :NZ]
        Z[f, x + 1, pl.ds(0, NY), :] = deep[NY:] + wide[:, NZ:]

    def advance(f, cur, prev, new, other, n):
        wait(f, cur, (n - 1) % 2)
        amp = jnp.broadcast_to(extra[n - 1, pl.ds(0, 8), pl.ds(32, 1)], (8, NZ))

        def planes(i, carry):
            x = 2 * i
            across(1 - f, cur if f == 0 else new, x)
            for j in range(NY // 8):
                crow = pl.ds(8 * j, 8)
                rows = crow
                wide = F[f, cur, pl.ds(x, 10), rows, :]
                u = wide[4:6]
                acc = Z[f, pl.ds(x, 2), crow, :]
                for k in range(1, 5):
                    acc = acc + WEIGHTS[k] * (wide[4 + k:6 + k] + wide[4 - k:6 - k])
                v = F[f, prev, pl.ds(4 + x, 2), rows, :]
                if f == 0:
                    force = E[pl.ds(x, 2), crow, :] * amp[None]
                else:
                    force = jnp.stack([pltpu.roll(T[x + h, crow, :], NZ - (8 - n), 1) * plane for h in range(2)])
                w = v + A[pl.ds(x, 2), crow, :] * ((u - v) + (C[pl.ds(x, 2), crow, :] * acc + force))
                F[f, new, pl.ds(4 + x, 2), rows, :] = w
                if other is not None:
                    image[pl.ds(x, 2), crow, :] += w * F[1 - f, other, pl.ds(4 + x, 2), rows, :]
            return carry

        for first, last, side in ((0, 2, 0), (14, 16, 1), (2, 14, None)):
            lax.fori_loop(first, last, planes, 0)
            if side is not None:
                @pl.when(n < 8)
                def _():
                    send(f, new, n % 2, side)

    def first_across(i, carry):
        across(0, 1, 2 * i)
        return carry

    lax.fori_loop(0, NX // 2, first_across, 0)

    def early(n, carry):
        for f in range(2):
            advance(f, n, n - 1, n + 1, None, n)
        return carry

    lax.fori_loop(1, 5, early, 0)

    def late(n, carry):
        for f in range(2):
            advance(f, n % 2 + 4 * (5 // n), (n - 1) % 2 + 4 * (6 // n), (n + 1) % 2, 10 - n, n)
        return carry

    lax.fori_loop(5, 9, late, 0)

    def store(j, carry):
        rows = pl.ds(pl.multiple_of(8 * j, 8), 8)
        for x in range(NX):
            out[pl.ds(8 * NX * j + x, 8, stride=NX), :] = image[x, rows, :] * 0.125
        return carry

    lax.fori_loop(0, NY // 8, store, 0)


def run_steps(fwd, adj, extra, speed, absorb):
    vm = pl.BlockSpec(memory_space=pltpu.VMEM)
    return pl.pallas_call(
        step_kernel,
        out_shape=jax.ShapeDtypeStruct((NY * NX, NZ), jnp.float32),
        in_specs=[vm] * 7,
        out_specs=vm,
        scratch_shapes=[
            pltpu.VMEM((2, 6, NX + 8, PY, NZ), jnp.float32),
            pltpu.VMEM((2, NX, PX, NZ), jnp.float32),
            pltpu.VMEM((NX, PX, NZ), jnp.float32),
            pltpu.VMEM((NX, PX, NZ), jnp.float32),
            pltpu.VMEM((NX, PX, NZ), jnp.float32),
            pltpu.VMEM((NX, PX, NZ), jnp.float32),
            pltpu.VMEM((NX, PX, NZ), jnp.float32),
            pltpu.SemaphoreType.DMA((2, 2, 2)),
            pltpu.SemaphoreType.DMA((2, 2, 2)),
        ],
        compiler_params=pltpu.CompilerParams(collective_id=1, has_side_effects=True, vmem_limit_bytes=62 << 20),
        name="wave_steps",
    )(fwd, adj, extra, speed, absorb, *band_pair())


def swap_pairs():
    pairs = []
    for s in range(16):
        for t in range(8):
            core, low = s % 2, t % 2
            pairs.append((s * 8 + t, (s - core + low) * 8 + (t - low + core)))
    return pairs


def body(courant, damping, aperture_block, source_cell, receiver_depth, wavelet, receiver_data,
         forward_state, adjoint_state):
    member = lax.axis_index("shot")
    first = aperture_block[member]
    axes = ("shot", "tile")
    pairs = swap_pairs()

    def swap(value):
        return lax.ppermute(value, axes, pairs)

    def window(model):
        whole = lax.all_gather(model, "shot", axis=0, tiled=True)
        return lax.dynamic_slice_in_dim(whole, first * 16, NY, 0)

    speed = window(courant).reshape(NY * NX, NZ)
    absorb = window(damping).reshape(NY * NX, NZ)
    records = jnp.pad(receiver_data[0], ((0, 0), (0, 0), (0, NZ - NX)))
    lane = lax.broadcasted_iota(jnp.int32, (8, NY, NZ), 2)
    extra = jnp.where(lane == 32, wavelet[0][:, None, None], records)
    extra = jnp.where(lane == 33, source_cell[0].astype(jnp.float32), extra)
    extra = jnp.where(lane == 34, receiver_depth[0].astype(jnp.float32), extra)
    partial = run_steps(
        swap(forward_state[0].reshape(2, NY * NX, NZ)), swap(adjoint_state[0].reshape(2, NY * NX, NZ)),
        swap(extra), swap(speed), swap(absorb))
    partial = swap(partial).reshape(NY, NX, NZ)
    whole = jnp.zeros((256, NX, NZ), jnp.float32)
    whole = lax.dynamic_update_slice_in_dim(whole, partial, first * 16, 0)
    return lax.psum_scatter(whole, "shot", scatter_dimension=0, tiled=True)


def solution(mesh):
    placed = (
        P("shot", "tile", None),
        P("shot", "tile", None),
        P(),
        P("shot"),
        P("shot"),
        P("shot", None),
        P("shot", None, None, "tile"),
        P("shot", None, None, "tile", None),
        P("shot", None, None, "tile", None),
    )
    return jax.shard_map(
        body, mesh=mesh, in_specs=placed, out_specs=P("shot", "tile", None), check_vma=False
    )
```

time: 577 us -> 356 us (0.62)
  other arithmetic: 138 us -> 0.13 us
  local copies, waits for them, and re-layouts: 89.5 us -> 9.85 us
  Pallas kernels: 0 us -> 76 us
  starting transfers between devices: 90.7 us -> 15.6 us
    pallas_call x0 -> x1, Pallas kernels: none -> 76 us  [run_steps(): pl.pallas_call(step_kernel, out_shape=jax.ShapeDtypeStruct((NY * NX, NZ),...]
    ppermute x32 -> x6, starting transfers between devices: 90.6 us -> 15.6 us  [swap(): return lax.ppermute(value, axes, pairs)]
    add x8 -> x0, other arithmetic: 64 us -> none  [backward(): return ((updated, current, summed + snapshot * updated), None)]
    dynamic_update_slice x8 -> x0, other arithmetic: 57.4 us -> none  [body(): lax.scan(forward, (forward_state[0, 0], forward_state[0, 1]), wavelet[0])]
    while x80 -> x0, local copies, waits for them, and re-layouts: 22.6 us -> none
    all_gather x2, waiting for transfers between devices: 100 us -> 118 us  [window(): whole = lax.all_gather(model, 'shot', axis=0, tiled=True)]
    ppermute x32 -> x6, waiting for transfers between devices: 54.2 us -> 37.7 us  [swap(): return lax.ppermute(value, axes, pairs)]
    slice x16 -> x0, local copies, waits for them, and re-layouts: 13 us -> none  [padded_2(): head = lax.slice_in_dim(cells, 0, width, axis=dim)]
  transfers between devices with their start and end apart: 35 -> 9, of which waited for: 22 -> 5; matrix products, arithmetic and copies ran while one was open for 8% -> 2% of each run, Pallas kernels for 0% -> 0%
where the time goes in v1:
time: 356 us; the launch traced here: 350 us
  waiting for transfers between devices  233 us (65%)
  Pallas kernels  76 us (21%)
  starting transfers between devices  15.6 us (4%)
  between operations  15.2 us (4%)
  local copies, waits for them, and re-layouts  9.85 us (3%)
    all_gather x2, waiting for transfers between devices, window(): whole = lax.all_gather(model, 'shot', axis=0, tiled=True)  118 us
    reduce_scatter x1, waiting for transfers between devices, body(): return lax.psum_scatter(whole, 'shot', scatter_dimension=0, tiled=True)  76.2 us
    pallas_call x1, Pallas kernels, run_steps(): pl.pallas_call(step_kernel, out_shape=jax.ShapeDtypeStruct((NY * NX, NZ),...  76 us
    ppermute x6, waiting for transfers between devices, swap(): return lax.ppermute(value, axes, pairs)  37.7 us
    ppermute x6, starting transfers between devices, swap(): return lax.ppermute(value, axes, pairs)  15.6 us
  transfers between devices with their start and end apart: 9, of which 5 were waited for; matrix products, arithmetic and copies ran while one was open for 2% of the time, Pallas kernels for 0%

profile of v1, /device:TPU:65, one launch (start us, length us, event | category | flops | bytes accessed | tf_op | source)
XLA Modules:
  0.0 349.7 jit_solution(10286391941049799297)
XLA Ops:
  6.5 0.0 all-gather.5.cloned.1.call-start
  6.5 0.7 all-gather.5.cloned.1.call-update
  7.3 0.0 all-gather.3.cloned.1.call-start
  7.3 0.7 all-gather.3.cloned.1.call-update
  8.0 0.0 reduce-scatter.2.cloned.1.call-start
  8.1 3.7 %collective-permute-start = (f32[2,3072,128]{2,1,0:T(8,128)}, f32[2,3072,128]{2,1,0:T(8,128)}, u32[]{:S(2)}, u32[]{:S(2)}) collective-permute-start(f32[2,3072,128]{2,1,0:T(8,128)} %bitcast.15), channel_id=1, source_target_pairs={{0,0},{1,8},{2,2},{3,10},{4,4},{5,12},{6,6},{7,14},{8,1},{9,9},{10... | collective-permute-start | bytes 9437192 | tf_op jit(solution)/shard_map/ppermute | solution.py:251
  11.7 1.9 collective-permute-start.1
  13.7 1.2 dynamic_slice.9
  15.6 0.0 copy-start.1
  15.6 58.7 %all-gather.5.cloned.1.call-done = f32[256,32,128]{2,1,0:T(8,128)} async-done(((f32[16,32,128]{2,1,0:T(8,128)}), f32[256,32,128]{2,1,0:T(8,128)}) %all-gather.5.cloned.1.call-update) | async-done | bytes 4194320 | tf_op jit(solution)/shard_map/all_gather | solution.py:254
  74.3 1.5 constant_dynamic-slice_fusion
  75.8 2.3 collective-permute-start.4
  78.2 58.9 %all-gather.3.cloned.1.call-done = f32[256,32,128]{2,1,0:T(8,128)} async-done(((f32[16,32,128]{2,1,0:T(8,128)}), f32[256,32,128]{2,1,0:T(8,128)}) %all-gather.3.cloned.1.call-update) | async-done | bytes 4194320 | tf_op jit(solution)/shard_map/all_gather | solution.py:254
  137.0 1.5 constant_dynamic-slice_fusion.1
  138.6 2.1 collective-permute-start.3
  141.9 1.1 copy.13
  143.0 0.0 copy-done.1
  143.0 0.1 select_select_fusion
  143.2 3.5 %collective-permute-start.2 = (f32[8,96,128]{2,1,0:T(8,128)S(1)}, f32[8,96,128]{2,1,0:T(8,128)S(1)}, u32[]{:S(2)}, u32[]{:S(2)}) collective-permute-start(f32[8,96,128]{2,1,0:T(8,128)S(1)} %select_select_fusion), channel_id=1, source_target_pairs={{0,0},{1,8},{2,2},{3,10},{4,4},{5,12},{6,6},{7,14},{8,1},{9,9},{10... | collective-permute-start | bytes 1179656 | tf_op jit(solution)/shard_map/ppermute | solution.py:251
  146.7 17.8 %collective-permute-done.2.extra = f32[8,96,128]{2,1,0:T(8,128)S(1)} collective-permute-done((f32[8,96,128]{2,1,0:T(8,128)S(1)}, f32[8,96,128]{2,1,0:T(8,128)S(1)}, u32[]{:S(2)}, u32[]{:S(2)}) %collective-permute-start.2) | collective-permute-done | bytes 393248 | tf_op jit(solution)/shard_map/ppermute | solution.py:251
  164.5 0.0 copy-start
  164.5 0.0 collective-permute-done.fwd
  164.5 0.0 collective-permute-done.1.adj
  164.5 0.0 collective-permute-done.4.absorb
  164.5 0.0 collective-permute-done.3.speed
  164.5 0.7 copy-done
  165.2 76.0 %wave_steps.1 = f32[3072,128]{1,0:T(8,128)} custom-call(f32[2,3072,128]{2,1,0:T(8,128)} %collective-permute-done.fwd, f32[2,3072,128]{2,1,0:T(8,128)} %collective-permute-done.1.adj, f32[8,96,128]{2,1,0:T(8,128)} %copy-done, f32[3072,128]{1,0:T(8,128)} %collective-permute-done.3.speed, f32[3072,128]{1,0:T(8,128)} %collective-permute-done.4.absorb, ...), custom_call_target="tpu_custom_call" | custom-call | tf_op jit(solution)/shard_map/wave_steps/pallas_call | solution.py:213
  241.2 2.1 collective-permute-start.5
  243.3 19.9 %collective-permute-done.5 = f32[3072,128]{1,0:T(8,128)S(1)} collective-permute-done((f32[3072,128]{1,0:T(8,128)}, f32[3072,128]{1,0:T(8,128)S(1)}, u32[]{:S(2)}, u32[]{:S(2)}) %collective-permute-start.5) | collective-permute-done | bytes 1572896 | tf_op jit(solution)/shard_map/ppermute | solution.py:251
  263.2 2.5 broadcast_in_dim.20
  265.7 1.3 constant_dynamic-update-slice_fusion
  267.0 0.0 reduce-scatter.2.cloned.1.call-update
  267.0 76.2 %reduce-scatter.2.cloned.1.call-done = f32[16,32,128]{2,1,0:T(8,128)} async-done(((f32[256,32,128]{2,1,0:T(8,128)}), f32[16,32,128]{2,1,0:T(8,128)}) %reduce-scatter.2.cloned.1.call-update) | async-done | bytes 262160 | tf_op jit(solution)/shard_map/reduce_scatter | solution.py:270
  (2 shorter events, 0.0 us)
Async XLA Ops:
  6.5 67.8 %all-gather.5.cloned.1.call-start = ((), (), s32[]{:S(2)}) async-start(), calls=%async_computation.2 | async-start | bytes 4456448 | tf_op jit(solution)/shard_map/all_gather | solution.py:254
  7.3 129.8 %all-gather.3.cloned.1.call-start = ((), (), s32[]{:S(2)}) async-start(), calls=%async_computation.1 | async-start | bytes 4456448 | tf_op jit(solution)/shard_map/all_gather | solution.py:254
  8.0 335.2 %reduce-scatter.2.cloned.1.call-start = ((), (), s32[]{:S(2)}) async-start(), calls=%async_computation.3 | async-start | bytes 4456448 | tf_op jit(solution)/shard_map/reduce_scatter | solution.py:270
  8.1 156.5 %collective-permute-start = (f32[2,3072,128]{2,1,0:T(8,128)}, f32[2,3072,128]{2,1,0:T(8,128)}, u32[]{:S(2)}, u32[]{:S(2)}) collective-permute-start(f32[2,3072,128]{2,1,0:T(8,128)} %bitcast.15), channel_id=1, source_target_pairs={{0,0},{1,8},{2,2},{3,10},{4,4},{5,12},{6,6},{7,14},{8,1},{9,9},{10... | collective-permute-start | bytes 9437192 | tf_op jit(solution)/shard_map/ppermute | solution.py:251
  11.7 152.8 %collective-permute-start.1 = (f32[2,3072,128]{2,1,0:T(8,128)}, f32[2,3072,128]{2,1,0:T(8,128)}, u32[]{:S(2)}, u32[]{:S(2)}) collective-permute-start(f32[2,3072,128]{2,1,0:T(8,128)} %bitcast.16), channel_id=1, source_target_pairs={{0,0},{1,8},{2,2},{3,10},{4,4},{5,12},{6,6},{7,14},{8,1},{9,9},{10... | collective-permute-start | bytes 9437192 | tf_op jit(solution)/shard_map/ppermute | solution.py:251
  15.6 127.5 %copy-start.1 = (f32[1,8]{1,0:T(1,128)S(1)}, f32[1,8]{1,0:T(1,128)}, u32[]{:S(2)}) copy-start(f32[1,8]{1,0:T(1,128)} %param.16) | copy-start | bytes 100
  75.8 88.7 %collective-permute-start.4 = (f32[3072,128]{1,0:T(8,128)S(1)}, f32[3072,128]{1,0:T(8,128)}, u32[]{:S(2)}, u32[]{:S(2)}) collective-permute-start(f32[3072,128]{1,0:T(8,128)S(1)} %bitcast.11), channel_id=1, source_target_pairs={{0,0},{1,8},{2,2},{3,10},{4,4},{5,12},{6,6},{7,14},{8,1},{9,9},{10... | collective-permute-start | bytes 4718600 | tf_op jit(solution)/shard_map/ppermute | solution.py:251
  138.6 26.0 %collective-permute-start.3 = (f32[3072,128]{1,0:T(8,128)S(1)}, f32[3072,128]{1,0:T(8,128)}, u32[]{:S(2)}, u32[]{:S(2)}) collective-permute-start(f32[3072,128]{1,0:T(8,128)S(1)} %bitcast.12), channel_id=1, source_target_pairs={{0,0},{1,8},{2,2},{3,10},{4,4},{5,12},{6,6},{7,14},{8,1},{9,9},{10... | collective-permute-start | bytes 4718600 | tf_op jit(solution)/shard_map/ppermute | solution.py:251
  143.2 21.4 %collective-permute-start.2 = (f32[8,96,128]{2,1,0:T(8,128)S(1)}, f32[8,96,128]{2,1,0:T(8,128)S(1)}, u32[]{:S(2)}, u32[]{:S(2)}) collective-permute-start(f32[8,96,128]{2,1,0:T(8,128)S(1)} %select_select_fusion), channel_id=1, source_target_pairs={{0,0},{1,8},{2,2},{3,10},{4,4},{5,12},{6,6},{7,14},{8,1},{9,9},{10... | collective-permute-start | bytes 1179656 | tf_op jit(solution)/shard_map/ppermute | solution.py:251
  164.5 0.7 copy-start
  241.2 21.9 %collective-permute-start.5 = (f32[3072,128]{1,0:T(8,128)}, f32[3072,128]{1,0:T(8,128)S(1)}, u32[]{:S(2)}, u32[]{:S(2)}) collective-permute-start(f32[3072,128]{1,0:T(8,128)} %wave_steps.1), channel_id=1, source_target_pairs={{0,0},{1,8},{2,2},{3,10},{4,4},{5,12},{6,6},{7,14},{8,1},{9,9},{10... | collective-permute-start | bytes 4718600 | tf_op jit(solution)/shard_map/ppermute | solution.py:251
Sparse Core Ops, SparseCore 0:
  9.8 64.4 all-gather.4
  76.8 60.2 all-gather.2
  267.1 76.0 reduce-scatter.1

commit v2 on v1

--- a/solution.py
+++ b/solution.py
@@ -14,6 +14,7 @@
 NY, NX, NZ = 96, 32, 128
 PY = 104
 PX = 104
+CHUNK = 128
 
 
 def band_matrix(size, centre):
@@ -29,7 +30,7 @@
             jnp.asarray(np.concatenate([wide, wide], axis=1), jnp.bfloat16))
 
 
-def step_kernel(fwd, adj, extra, speed, absorb, band_z, band_y, out, F, Z, A, C, E, T, image, ssem, rsem):
+def step_kernel(fwd, adj, extra, window, band_z, band_y, out, F, Z, A, C, E, T, image, ssem, rsem):
     s = lax.axis_index("shot")
     t = lax.axis_index("tile")
     core = s % 2
@@ -125,8 +126,8 @@
                 value = jnp.broadcast_to(extra[m, rows, pl.ds(x, 1)], (8, NZ))
                 placed = jnp.where(lane.astype(jnp.float32) == turns[m], value, placed)
             T[x, rows, :] = placed
-            A[x, rows, :] = 2.0 / (1.0 + absorb[picked, :])
-            C[x, rows, :] = speed[picked, :] * (0.5 / SCALE)
+            A[x, rows, :] = 2.0 / (1.0 + window[1, picked, :])
+            C[x, rows, :] = window[0, picked, :] * (0.5 / SCALE)
             index = (place * NX + x) * (NY * NZ) + (row + 8 * j) * NZ + lane
             E[x, rows, :] = jnp.where(index.astype(jnp.float32) == cell, 0.5, 0.0)
             image[x, rows, :] = jnp.zeros((8, NZ), jnp.float32)
@@ -208,12 +209,12 @@
     lax.fori_loop(0, NY // 8, store, 0)
 
 
-def run_steps(fwd, adj, extra, speed, absorb):
+def run_steps(fwd, adj, extra, window):
     vm = pl.BlockSpec(memory_space=pltpu.VMEM)
     return pl.pallas_call(
         step_kernel,
         out_shape=jax.ShapeDtypeStruct((NY * NX, NZ), jnp.float32),
-        in_specs=[vm] * 7,
+        in_specs=[vm] * 6,
         out_specs=vm,
         scratch_shapes=[
             pltpu.VMEM((2, 6, NX + 8, PY, NZ), jnp.float32),
@@ -228,46 +229,268 @@
         ],
         compiler_params=pltpu.CompilerParams(collective_id=1, has_side_effects=True, vmem_limit_bytes=62 << 20),
         name="wave_steps",
-    )(fwd, adj, extra, speed, absorb, *band_pair())
-
-
-def swap_pairs():
-    pairs = []
-    for s in range(16):
-        for t in range(8):
-            core, low = s % 2, t % 2
-            pairs.append((s * 8 + t, (s - core + low) * 8 + (t - low + core)))
-    return pairs
+    )(fwd, adj, extra, window, *band_pair())
+
+
+def position():
+    s = lax.axis_index("shot")
+    t = lax.axis_index("tile")
+    return s // 8, (s // 2) % 4, s % 2, t // 2, t % 2
+
+
+def device(xh, y, core, z, xl):
+    return (xh * 8 + y * 2 + core, z * 2 + xl)
+
+
+def meet(xh, y, core, z, xl):
+    barrier = pltpu.get_barrier_semaphore()
+    peers = []
+    for a in range(2):
+        for b in range(2):
+            for e in range(2):
+                if a or b or e:
+                    peers.append(device((xh + a) % 2, y, (core + b) % 2, z, (xl + e) % 2))
+    for d in range(1, 4):
+        peers.append(device(xh, (y + d) % 4, core, z, xl))
+    for peer in peers:
+        pl.semaphore_signal(barrier, inc=1, device_id=peer, device_id_type=MESH_ID)
+    pl.semaphore_wait(barrier, len(peers))
+
+
+def gather_kernel(blocks, model, fwd, adj, extra, fwd_out, adj_out, extra_out, window,
+                  line, packed, ring, xsend, xrecv, fsend, ysend, yrecv, ssend, srecv, local):
+    xh, y, core, z, xl = position()
+    meet(xh, y, core, z, xl)
+    away = core != xl
+    home = core == xl
+
+    def remote(source, target, send, recv, peer):
+        return pltpu.make_async_remote_copy(src_ref=source, dst_ref=target, send_sem=send, recv_sem=recv,
+                                            device_id=peer, device_id_type=MESH_ID)
+
+    def own(k, peer):
+        return remote(model, line.at[xh, core], xsend.at[k], xrecv.at[xh, core], peer)
+
+    cross = own(0, device(1 - xh, y, xl, z, 1 - xl))
+    pair = own(1, device(xh, y, xl, z, 1 - xl))
+    inside = own(2, device(xh, y, 1 - core, z, xl))
+    keep = pltpu.make_async_copy(model, line.at[xh, core], local.at[0])
+    pair.start()
+    cross.start()
+    pl.when(away)(inside.start)
+    pl.when(home)(keep.start)
+
+    partner = device(xh, y, xl, z, core)
+    moves = []
+    for k, (source, target) in enumerate(((fwd, fwd_out), (adj, adj_out), (extra, extra_out))):
+        moves.append((remote(source, target, ssend.at[k], srecv.at[k], partner),
+                      pltpu.make_async_copy(source, target, local.at[1 + k])))
+    for far, near in moves:
+        pl.when(away)(far.start)
+        pl.when(home)(near.start)
+
+    def arrived(a, b):
+        remote(line.at[a, b], line.at[a, b], xsend.at[0], xrecv.at[a, b], partner).wait_recv()
+
+    def forward(b):
+        return remote(line.at[xh, b], line.at[xh, b], fsend.at[b], xrecv.at[xh, b],
+                      device(1 - xh, y, core, z, 1 - xl))
+
+    @pl.when(away)
+    def _():
+        for b in range(2):
+            arrived(xh, b)
+            forward(b).start()
+
+    @pl.when(home)
+    def _():
+        keep.wait()
+        arrived(xh, 1 - core)
+
+    for b in range(2):
+        arrived(1 - xh, b)
+
+    def pick(target, d):
+        first = blocks[xh * 8 + ((y + d) % 4) * 2 + xl]
+        for b in range(2):
+            half = (2 * y + b < first).astype(jnp.int32)
+
+            def rows(i, carry):
+                part = pl.ds(pl.multiple_of(64 * i, 64), 64)
+                target[b, :, part, :] = line[half, b, :, part, :]
+                return carry
+            lax.fori_loop(0, 8, rows, 0)
+
+    def round_trip(d):
+        return remote(packed.at[d - 1], ring.at[d], ysend.at[d - 1], yrecv.at[d - 1],
+                      device(xh, (y + d) % 4, core, z, xl))
+
+    for d in (2, 1, 3):
+        pick(packed.at[d - 1], d)
+        round_trip(d).start()
+    pick(ring.at[0], 0)
+    for d in (1, 3, 2):
+        round_trip(d).wait()
+
+    first = blocks[xh * 8 + y * 2 + xl]
+    for k in range(6):
+        j = first + k
+        place = (y - (j // 2) % 4 + 4) % 4
+        parity = j % 2
+
+        def rows(i, carry):
+            part = pl.ds(pl.multiple_of(64 * i, 64), 64)
+            window[:, pl.ds(pl.multiple_of(512 * k + 64 * i, 64), 64), :] = ring[place, parity, :, part, :]
+            return carry
+        lax.fori_loop(0, 8, rows, 0)
+
+    pair.wait_send()
+    cross.wait_send()
+
+    @pl.when(away)
+    def _():
+        inside.wait_send()
+        for b in range(2):
+            forward(b).wait_send()
+        for far, near in moves:
+            far.wait()
+
+    @pl.when(home)
+    def _():
+        for far, near in moves:
+            near.wait()
+
+
+def run_gather(blocks, model, fwd, adj, extra):
+    vm = pl.BlockSpec(memory_space=pltpu.VMEM)
+    anywhere = pl.BlockSpec(memory_space=pl.ANY)
+    like = lambda v: jax.ShapeDtypeStruct(v.shape, v.dtype)
+    dma = pltpu.SemaphoreType.DMA
+    return pl.pallas_call(
+        gather_kernel,
+        out_shape=[like(fwd), like(adj), like(extra), jax.ShapeDtypeStruct((2, NY * NX, NZ), jnp.float32)],
+        in_specs=[pl.BlockSpec(memory_space=pltpu.SMEM)] + [anywhere] * 4,
+        out_specs=[anywhere] * 3 + [vm],
+        scratch_shapes=[
+            pltpu.VMEM((2, 2, 2, 512, NZ), jnp.float32),
+            pltpu.VMEM((3, 2, 2, 512, NZ), jnp.float32),
+            pltpu.VMEM((4, 2, 2, 512, NZ), jnp.float32),
+            dma((3,)), dma((2, 2)), dma((2,)), dma((3,)), dma((3,)), dma((3,)), dma((3,)), dma((4,)),
+        ],
+        compiler_params=pltpu.CompilerParams(collective_id=2, has_side_effects=True, vmem_limit_bytes=24 << 20),
+        name="place",
+    )(blocks, model, fwd, adj, extra)
+
+
+def sum_kernel(blocks, partial, out, packed, ring, totals, line, ysend, yrecv, xsend, xrecv):
+    xh, y, core, z, xl = position()
+    meet(xh, y, core, z, xl)
+
+    def choose(first, row, b):
+        half = (2 * row + b < first).astype(jnp.int32)
+        step = 8 * half + 2 * row + b - first
+        inside = (step >= 0).astype(jnp.int32) * (step < 6).astype(jnp.int32)
+        return half + 2 * (1 - inside), step
+
+    def turn(d, q):
+        return pltpu.make_async_remote_copy(
+            src_ref=packed.at[q, d - 1], dst_ref=ring.at[q, d], send_sem=ysend.at[q, d - 1], recv_sem=yrecv.at[q, d - 1],
+            device_id=device(xh, (y + d) % 4, core, z, xl), device_id_type=MESH_ID)
+
+    def pick(target, d, q):
+        first = blocks[xh * 8 + y * 2 + xl]
+        for b in range(2):
+            half, step = choose(first, (y + d) % 4, b)
+            target[b] = partial[jnp.clip(step, 0, 5), pl.ds(CHUNK * q, CHUNK), :]
+
+    for q in range(512 // CHUNK):
+        for d in (2, 1, 3):
+            pick(packed.at[q, d - 1], d, q)
+            turn(d, q).start()
+        pick(ring.at[q, 0], 0, q)
+
+    def spread(k, q):
+        a, b = k // 2, k % 2
+        return pltpu.make_async_remote_copy(
+            src_ref=totals.at[q, k], dst_ref=line.at[q, xh * 2 + xl], send_sem=xsend.at[q, k],
+            recv_sem=xrecv.at[q, xh * 2 + xl], device_id=device(a, y, b, z, core), device_id_type=MESH_ID)
+
+    def mine(k):
+        return (xh == k // 2) & (core == k % 2) & (xl == core)
+
+    for q in range(512 // CHUNK):
+        for d in (1, 3, 2):
+            turn(d, q).wait_recv()
+        for k in range(4):
+            a, b = k // 2, k % 2
+            total = jnp.zeros((CHUNK, NZ), jnp.float32)
+            for d in range(4):
+                first = blocks[xh * 8 + ((y - d + 4) % 4) * 2 + xl]
+                half, step = choose(first, y, b)
+                total = total + jnp.where(jnp.full((CHUNK, NZ), half, jnp.int32) == a, ring[q, d, b], 0.0)
+            totals[q, k] = total
+
+            @pl.when(jnp.logical_not(mine(k)))
+            def _():
+                spread(k, q).start()
+
+            @pl.when(mine(k))
+            def _():
+                line[q, xh * 2 + xl] = totals[q, k]
+
+    for q in range(512 // CHUNK):
+        for k in range(4):
+            source = device(k // 2, y, xl, z, k % 2)
+
+            @pl.when(jnp.logical_not((xh * 2 + xl == k) & (xl == core)))
+            def _():
+                pltpu.make_async_remote_copy(
+                    src_ref=line.at[q, k], dst_ref=line.at[q, k], send_sem=xsend.at[q, k], recv_sem=xrecv.at[q, k],
+                    device_id=source, device_id_type=MESH_ID).wait_recv()
+        out[pl.ds(CHUNK * q, CHUNK), :] = (line[q, 0] + line[q, 1]) + (line[q, 2] + line[q, 3])
+
+    for q in range(512 // CHUNK):
+        for d in (1, 3, 2):
+            turn(d, q).wait_send()
+        for k in range(4):
+            @pl.when(jnp.logical_not(mine(k)))
+            def _():
+                spread(k, q).wait_send()
+
+
+def run_sum(blocks, partial):
+    vm = pl.BlockSpec(memory_space=pltpu.VMEM)
+    dma = pltpu.SemaphoreType.DMA
+    count = 512 // CHUNK
+    return pl.pallas_call(
+        sum_kernel,
+        out_shape=jax.ShapeDtypeStruct((512, NZ), jnp.float32),
+        in_specs=[pl.BlockSpec(memory_space=pltpu.SMEM), vm],
+        out_specs=vm,
+        scratch_shapes=[
+            pltpu.VMEM((count, 3, 2, CHUNK, NZ), jnp.float32),
+            pltpu.VMEM((count, 4, 2, CHUNK, NZ), jnp.float32),
+            pltpu.VMEM((count, 4, CHUNK, NZ), jnp.float32),
+            pltpu.VMEM((count, 4, CHUNK, NZ), jnp.float32),
+            dma((count, 3)), dma((count, 3)), dma((count, 4)), dma((count, 4)),
+        ],
+        compiler_params=pltpu.CompilerParams(collective_id=3, has_side_effects=True, vmem_limit_bytes=24 << 20),
+        name="image_sum",
+    )(blocks, partial)
 
 
 def body(courant, damping, aperture_block, source_cell, receiver_depth, wavelet, receiver_data,
          forward_state, adjoint_state):
-    member = lax.axis_index("shot")
-    first = aperture_block[member]
-    axes = ("shot", "tile")
-    pairs = swap_pairs()
-
-    def swap(value):
-        return lax.ppermute(value, axes, pairs)
-
-    def window(model):
-        whole = lax.all_gather(model, "shot", axis=0, tiled=True)
-        return lax.dynamic_slice_in_dim(whole, first * 16, NY, 0)
-
-    speed = window(courant).reshape(NY * NX, NZ)
-    absorb = window(damping).reshape(NY * NX, NZ)
     records = jnp.pad(receiver_data[0], ((0, 0), (0, 0), (0, NZ - NX)))
     lane = lax.broadcasted_iota(jnp.int32, (8, NY, NZ), 2)
     extra = jnp.where(lane == 32, wavelet[0][:, None, None], records)
     extra = jnp.where(lane == 33, source_cell[0].astype(jnp.float32), extra)
     extra = jnp.where(lane == 34, receiver_depth[0].astype(jnp.float32), extra)
-    partial = run_steps(
-        swap(forward_state[0].reshape(2, NY * NX, NZ)), swap(adjoint_state[0].reshape(2, NY * NX, NZ)),
-        swap(extra), swap(speed), swap(absorb))
-    partial = swap(partial).reshape(NY, NX, NZ)
-    whole = jnp.zeros((256, NX, NZ), jnp.float32)
-    whole = lax.dynamic_update_slice_in_dim(whole, partial, first * 16, 0)
-    return lax.psum_scatter(whole, "shot", scatter_dimension=0, tiled=True)
+    model = jnp.stack([courant.reshape(512, NZ), damping.reshape(512, NZ)])
+    fwd, adj, extra, window = run_gather(
+        aperture_block, model, forward_state[0].reshape(2, NY * NX, NZ), adjoint_state[0].reshape(2, NY * NX, NZ), extra)
+    partial = run_steps(fwd, adj, extra, window).reshape(6, 512, NZ)
+    return run_sum(aperture_block, partial).reshape(16, NX, NZ)
 
 
 def solution(mesh):

time: 356 us -> 218 us (0.61); the launches traced: 350 us -> 217 us
  waiting for transfers between devices: 233 us -> 0 us
  Pallas kernels: 76 us -> 200 us
  starting transfers between devices: 15.6 us -> 0 us
  between operations: 15.2 us -> 1.39 us
    pallas_call x0 -> x2, Pallas kernels: none -> 124 us  [the longest x1 88.8 us: run_gather(): pl.pallas_call(gather_kernel, out_shape=[like(fwd), like(adj), like(extra...]
    all_gather x2 -> x0, waiting for transfers between devices: 118 us -> none  [window(): whole = lax.all_gather(model, 'shot', axis=0, tiled=True)]
    reduce_scatter x1 -> x0, waiting for transfers between devices: 76.2 us -> none  [body(): return lax.psum_scatter(whole, 'shot', scatter_dimension=0, tiled=True)]
    ppermute x6 -> x0, waiting for transfers between devices: 37.7 us -> none  [swap(): return lax.ppermute(value, axes, pairs)]
    ppermute x6 -> x0, starting transfers between devices: 15.6 us -> none  [swap(): return lax.ppermute(value, axes, pairs)]
    unnamed x5 -> x20, local copies, waits for them, and re-layouts: 1.79 us -> 13.4 us
    dynamic_slice x3 -> x0, local copies, waits for them, and re-layouts: 4.29 us -> none  [the longest x2 3.05 us: window(): return lax.dynamic_slice_in_dim(whole, first * 16, NY, 0)]
  transfers between devices with their start and end apart: 9 -> 0, of which waited for: 5 -> 0; matrix products, arithmetic and copies ran while one was open for 2% -> 0% of each run, Pallas kernels for 0% -> 0%
where the time goes in v2:
time: 218 us; the launch traced here: 217 us
  Pallas kernels  200 us (92%)
  local copies, waits for them, and re-layouts  13.4 us (6%)
    pallas_call x1, Pallas kernels, run_gather(): pl.pallas_call(gather_kernel, out_shape=[like(fwd), like(adj), like(extra...  88.8 us
    pallas_call x1, Pallas kernels, run_steps(): pl.pallas_call(step_kernel, out_shape=jax.ShapeDtypeStruct((NY * NX, NZ),...  75.9 us
    pallas_call x1, Pallas kernels, run_sum(): pl.pallas_call(sum_kernel, out_shape=jax.ShapeDtypeStruct((512, NZ), jnp....  35.4 us
    unnamed x20, local copies, waits for them, and re-layouts  13.4 us

profile of v2, /device:TPU:65, one launch (start us, length us, event | category | flops | bytes accessed | tf_op | source)
XLA Modules:
  0.0 216.7 jit_solution(8338029724452967767)
XLA Ops:
  1.3 1.1 copy.12
  2.4 0.8 select_select_fusion.extra
  3.2 1.1 pad_maximum_fusion.model
  4.3 0.0 copy-start.1
  4.3 1.9 copy-done.1
  6.1 0.0 copy-start.2
  6.1 1.9 copy-done.2
  8.0 0.0 copy-start.7
  8.0 0.7 copy-done.7
  8.7 88.8 %place.1 = (f32[2,3072,128]{2,1,0:T(8,128)S(1)}, f32[2,3072,128]{2,1,0:T(8,128)S(1)}, f32[8,96,128]{2,1,0:T(8,128)S(1)}, f32[2,3072,128]{2,1,0:T(8,128)S(1)}) custom-call(s32[16]{0:T(128)S(1)} %copy-done.7, f32[2,512,128]{2,1,0:T(8,128)S(1)} %pad_maximum_fusion.model, f32[2,3072,128]{2,1,0:T(8,128)S(1)} %bitcast.11, f32[2,3072,128]{2,1,0:T(8,128)S(1)} %bitcast.12, ...), custom_call_target="tpu_custom_call" | custom-call | tf_op jit(solution)/shard_map/place/pallas_call | solution.py:369
  97.5 0.0 copy-start.3
  97.5 1.6 copy-done.3
  99.1 0.0 copy-start.4
  99.1 1.7 copy-done.4
  100.8 0.0 copy-start.5
  100.8 1.7 copy-done.5
  102.5 0.0 copy-start.6
  102.5 0.8 copy-done.6
  103.3 0.0 copy-start.8
  103.3 75.9 %wave_steps.1 = f32[3072,128]{1,0:T(8,128)} custom-call(f32[2,3072,128]{2,1,0:T(8,128)} %copy-done.3, f32[2,3072,128]{2,1,0:T(8,128)} %copy-done.4, f32[8,96,128]{2,1,0:T(8,128)} %copy-done.6, f32[2,3072,128]{2,1,0:T(8,128)} %copy-done.5, bf16[256,128]{1,0:T(8,128)(2,1)} %constant.13.clone.band_z, bf16[96,192]{1,0:T(8,128)(2,1)} %constant.14.clone.band_y), custom_call_target="tpu_custom_call" | custom-call | tf_op jit(solution)/shard_map/wave_steps/pallas_call | solution.py:214
  179.2 0.0 copy-done.8
  179.2 0.0 copy-start
  179.2 1.4 copy-done
  180.6 35.4 %image_sum.1 = f32[512,128]{1,0:T(8,128)S(1)} custom-call(s32[16]{0:T(128)S(1)} %copy-done.8, f32[6,512,128]{2,1,0:T(8,128)S(1)} %bitcast.10), custom_call_target="tpu_custom_call" | custom-call | tf_op jit(solution)/shard_map/image_sum/pallas_call | solution.py:465
  216.0 0.7 copy.16
  (2 shorter events, 0.0 us)
Async XLA Ops:
  4.3 1.9 copy-start.1
  6.1 1.9 copy-start.2
  8.0 0.7 copy-start.7
  97.5 1.6 copy-start.3
  99.1 1.7 copy-start.4
  100.8 1.7 copy-start.5
  102.5 0.8 copy-start.6
  103.3 75.9 %copy-start.8 = (s32[16]{0:T(128)S(1)}, s32[16]{0:T(128)}, u32[]{:S(2)}) copy-start(s32[16]{0:T(128)} %blocks.3) | copy-start | bytes 196
  179.2 1.4 copy-start

commit v3 on v2

v3 whole, which is shorter than its diff:
```python
import functools
import jax
import jax.numpy as jnp
import numpy as np
from jax import lax
from jax.experimental import pallas as pl
from jax.experimental.pallas import tpu as pltpu
from jax.sharding import PartitionSpec as P

MESH_ID = pl.DeviceIdType.MESH
SCALE = 5040.0
WEIGHTS = (-43050.0, 8064.0, -1008.0, 128.0, -9.0)
CENTRES = (-43008.0, -42.0)
NY, NX, NZ = 96, 32, 128
PY = 104
PX = 104
WIDE = 4
CHUNK = 128


def band_matrix(size, centre):
    band = centre * np.eye(size, dtype=np.float32)
    for offset in range(1, 5):
        band += WEIGHTS[offset] * (np.eye(size, k=offset) + np.eye(size, k=-offset))
    return band


def band_pair():
    deep, wide = band_matrix(NZ, CENTRES[0]), band_matrix(NY, CENTRES[1])
    deep = np.kron(np.eye(2, dtype=np.float32), deep)
    return (jnp.asarray(np.concatenate([deep, deep], axis=0), jnp.bfloat16),
            jnp.asarray(np.concatenate([wide, wide], axis=1), jnp.bfloat16))


def position():
    s = lax.axis_index("shot")
    t = lax.axis_index("tile")
    return s // 8, (s // 2) % 4, s % 2, t // 2, t % 2


def device(xh, y, core, z, xl):
    return (xh * 8 + y * 2 + core, z * 2 + xl)


def meet(xh, y, core, z, xl, more=None, wanted=None):
    barrier = pltpu.get_barrier_semaphore()
    peers = []
    for a in range(2):
        for b in range(2):
            for e in range(2):
                if a or b or e:
                    peers.append(device((xh + a) % 2, y, (core + b) % 2, z, (xl + e) % 2))
    for d in range(1, 4):
        peers.append(device(xh, (y + d) % 4, core, z, xl))
    for peer in peers:
        pl.semaphore_signal(barrier, inc=1, device_id=peer, device_id_type=MESH_ID)
    if more is None:
        pl.semaphore_wait(barrier, len(peers))
    else:
        @pl.when(wanted)
        def _():
            pl.semaphore_signal(barrier, inc=1, device_id=more, device_id_type=MESH_ID)
        pl.semaphore_wait(barrier, len(peers) + wanted.astype(jnp.int32))


def wave_kernel(blocks, model, fwd, adj, extra_in, band_z, band_y, out, *scratch):
    fields = (scratch[0:6], scratch[6:12])
    Z = scratch[12:14]
    (A, C, E, T, image, raw_f, raw_a, extra, line, packed, ring, ssem, rsem,
     xsend, xrecv, fsend, ysend, yrecv, msend, mrecv, local) = scratch[14:]
    xh, y, core, z, xl = position()
    place = 2 * z + core
    has_left = place > 0
    has_right = place < 7
    left = device(xh, y, 1 - core, z - 1 + core, xl)
    right = device(xh, y, 1 - core, z + core, xl)
    beyond = device(xh, y, 1 - core, z - 1 + 2 * core, xl)
    meet(xh, y, core, z, xl, beyond, (z - 1 + 2 * core >= 0) & (z - 1 + 2 * core < 4))
    away = core != xl
    home = core == xl

    def remote(source, target, send, recv, peer):
        return pltpu.make_async_remote_copy(src_ref=source, dst_ref=target, send_sem=send, recv_sem=recv,
                                            device_id=peer, device_id_type=MESH_ID)

    def own(k, peer):
        return remote(model, line.at[xh, core], xsend.at[k], xrecv.at[xh, core], peer)

    cross = own(0, device(1 - xh, y, xl, z, 1 - xl))
    pair = own(1, device(xh, y, xl, z, 1 - xl))
    inside = own(2, device(xh, y, 1 - core, z, xl))
    keep = pltpu.make_async_copy(model, line.at[xh, core], local.at[0])
    pair.start()
    cross.start()
    pl.when(away)(inside.start)
    pl.when(home)(keep.start)

    partner = device(xh, y, xl, z, core)
    moves = []
    for k, (source, target) in enumerate(((extra_in, extra), (fwd, raw_f), (adj, raw_a))):
        moves.append((remote(source, target, msend.at[k], mrecv.at[k], partner),
                      pltpu.make_async_copy(source, target, local.at[1 + k])))
    for far, near in moves:
        pl.when(away)(far.start)
        pl.when(home)(near.start)

    def arrived(a, b):
        remote(line.at[a, b], line.at[a, b], xsend.at[0], xrecv.at[a, b], partner).wait_recv()

    def forward(b):
        return remote(line.at[xh, b], line.at[xh, b], fsend.at[b], xrecv.at[xh, b],
                      device(1 - xh, y, core, z, 1 - xl))

    @pl.when(away)
    def _():
        for b in range(2):
            arrived(xh, b)
            forward(b).start()

    @pl.when(home)
    def _():
        keep.wait()
        arrived(xh, 1 - core)

    for b in range(2):
        arrived(1 - xh, b)

    def pick(target, d):
        first = blocks[xh * 8 + ((y + d) % 4) * 2 + xl]
        for b in range(2):
            half = (2 * y + b < first).astype(jnp.int32)

            def rows(i, carry):
                part = pl.ds(pl.multiple_of(64 * i, 64), 64)
                target[b, :, part, :] = line[half, b, :, part, :]
                return carry
            lax.fori_loop(0, 8, rows, 0)

    def round_trip(d):
        return remote(packed.at[d - 1], ring.at[d], ysend.at[d - 1], yrecv.at[d - 1],
                      device(xh, (y + d) % 4, core, z, xl))

    for d in (2, 1, 3):
        pick(packed.at[d - 1], d)
        round_trip(d).start()
    def landed(i):
        far, near = moves[i]
        pl.when(away)(far.wait_recv)
        pl.when(home)(near.wait)

    def halo(f, slot, par, side):
        if side == 0:
            return pltpu.make_async_remote_copy(
                src_ref=fields[f][slot].at[pl.ds(4, 4), pl.ds(0, NY), :],
                dst_ref=fields[f][slot].at[pl.ds(36, 4), pl.ds(0, NY), :],
                send_sem=ssem.at[f, 0, par], recv_sem=rsem.at[f, 0, par],
                device_id=left, device_id_type=MESH_ID)
        return pltpu.make_async_remote_copy(
            src_ref=fields[f][slot].at[pl.ds(32, 4), pl.ds(0, NY), :],
            dst_ref=fields[f][slot].at[pl.ds(0, 4), pl.ds(0, NY), :],
            send_sem=ssem.at[f, 1, par], recv_sem=rsem.at[f, 1, par],
            device_id=right, device_id_type=MESH_ID)

    def send(f, slot, par, side):
        @pl.when(has_left if side == 0 else has_right)
        def _():
            halo(f, slot, par, side).start()

    def wait(f, slot, par):
        @pl.when(has_left)
        def _():
            halo(f, slot, par, 0).wait_send()
            halo(f, slot, par, 1).wait_recv()

        @pl.when(has_right)
        def _():
            halo(f, slot, par, 1).wait_send()
            halo(f, slot, par, 0).wait_recv()

    zero_side = jnp.zeros((4, NY, NZ), jnp.float32)

    @pl.when(place == 0)
    def _():
        for f in range(2):
            for slot in range(6):
                fields[f][slot][pl.ds(0, 4), pl.ds(0, NY), :] = zero_side

    @pl.when(place == 7)
    def _():
        for f in range(2):
            for slot in range(6):
                fields[f][slot][pl.ds(36, 4), pl.ds(0, NY), :] = zero_side

    landed(0)
    lane = lax.broadcasted_iota(jnp.int32, (8, NZ), 1)
    row = lax.broadcasted_iota(jnp.int32, (8, NZ), 0)
    depth = jnp.broadcast_to(extra[pl.ds(192, 8), pl.ds(9, 1)], (8, NZ))
    plane = jnp.where(lane.astype(jnp.float32) == depth, 0.5, 0.0)
    cell = jnp.broadcast_to(extra[pl.ds(192, 8), pl.ds(8, 1)], (8, NZ))
    turns = [(depth + m) - jnp.where(depth + m >= NZ, float(NZ), 0.0) for m in range(8)]

    def load_extra(j, carry):
        rows = pl.ds(pl.multiple_of(8 * j, 8), 8)
        records = [extra[pl.ds(pl.multiple_of(NY * h + 8 * j, 8), 8), :] for h in range(2)]
        for x in range(NX):
            placed = jnp.zeros((8, NZ), jnp.float32)
            for m in range(8):
                at = (m % 4) * NX + x
                value = jnp.broadcast_to(records[m // 4][:, at:at + 1], (8, NZ))
                placed = jnp.where(lane.astype(jnp.float32) == turns[m], value, placed)
            T[x, rows, :] = placed
            index = (place * NX + x) * (NY * NZ) + (row + 8 * j) * NZ + lane
            E[x, rows, :] = jnp.where(index.astype(jnp.float32) == cell, 0.5, 0.0)
            image[x, rows, :] = jnp.zeros((8, NZ), jnp.float32)
        return carry

    lax.fori_loop(0, NY // 8, load_extra, 0)

    def load_states(f, source):
        def tiles(j, carry):
            rows = pl.ds(pl.multiple_of(8 * j, 8), 8)
            for x in range(NX):
                picked = pl.ds(8 * NX * j + x, 8, stride=NX)
                fields[f][1][4 + x, rows, :] = source[0, picked, :]
                fields[f][0][4 + x, rows, :] = source[1, picked, :]
            return carry
        lax.fori_loop(0, NY // 8, tiles, 0)
        send(f, 1, 0, 0)
        send(f, 1, 0, 1)

    def across(f, slot, x):
        for h in range(0, WIDE, 2):
            u = fields[f][slot][pl.ds(4 + x + h, 2), pl.ds(0, NY), :]
            high = u.astype(jnp.bfloat16)
            low = (u - high.astype(jnp.float32)).astype(jnp.bfloat16)
            high = jnp.concatenate([high[0], high[1]], axis=1)
            low = jnp.concatenate([low[0], low[1]], axis=1)
            rows = jnp.concatenate([high, low, band_y[...]], axis=1)
            columns = jnp.concatenate([band_z[...], high, low], axis=0)
            both = jnp.dot(rows, columns, preferred_element_type=jnp.float32)
            Z[f][x + h, pl.ds(0, NY), :] = both[:, :NZ]
            Z[f][x + h + 1, pl.ds(0, NY), :] = both[:, NZ:]

    def slot_of(n):
        return n + 1 if n < 5 else (n + 1) % 2

    def advance(f, n):
        cur, prev, new = fields[f][slot_of(n - 1)], fields[f][slot_of(n - 2)], fields[f][slot_of(n)]
        other = fields[1 - f][slot_of(9 - n)] if n > 4 else None
        wait(f, slot_of(n - 1), (n - 1) % 2)
        amp = jnp.broadcast_to(extra[pl.ds(192, 8), pl.ds(n - 1, 1)], (8, NZ))

        def planes(i, carry):
            x = WIDE * i
            if f == 0 and n > 1:
                across(1, slot_of(n - 1), x)
            if f == 1 and n < 8:
                across(0, slot_of(n), x)
            for j in range(NY // 8):
                rows = pl.ds(8 * j, 8)
                wide = cur[pl.ds(x, WIDE + 8), rows, :]
                u = wide[4:4 + WIDE]
                acc = Z[f][pl.ds(x, WIDE), rows, :]
                for k in range(1, 5):
                    acc = acc + WEIGHTS[k] * (wide[4 + k:4 + k + WIDE] + wide[4 - k:4 - k + WIDE])
                v = prev[pl.ds(4 + x, WIDE), rows, :]
                if f == 0:
                    force = E[pl.ds(x, WIDE), rows, :] * amp[None]
                else:
                    force = jnp.stack([pltpu.roll(T[x + h, rows, :], NZ - (8 - n), 1) * plane for h in range(WIDE)])
                w = v + A[pl.ds(x, WIDE), rows, :] * ((u - v) + (C[pl.ds(x, WIDE), rows, :] * acc + force))
                new[pl.ds(4 + x, WIDE), rows, :] = w
                if other is not None:
                    image[pl.ds(x, WIDE), rows, :] += w * other[pl.ds(4 + x, WIDE), rows, :]
            return carry

        for first, last, side in ((0, 4 // WIDE, 0), (28 // WIDE, 32 // WIDE, 1), (4 // WIDE, 28 // WIDE, None)):
            lax.fori_loop(first, last, planes, 0)
            if side is not None and n < 8:
                send(f, slot_of(n), n % 2, side)

    def first_across(f):
        def planes(i, carry):
            across(f, 1, WIDE * i)
            return carry
        lax.fori_loop(0, NX // WIDE, planes, 0)

    landed(1)
    load_states(0, raw_f)
    first_across(0)
    pick(ring.at[0], 0)
    for d in (1, 3, 2):
        round_trip(d).wait()


    first = blocks[xh * 8 + y * 2 + xl]

    def load_model(k, carry):
        j = first + k
        turn = (y - (j // 2) % 4 + 4) % 4
        parity = j % 2
        for h in range(2):
            rows = pl.ds(pl.multiple_of(16 * k + 8 * h, 8), 8)
            for x in range(NX):
                picked = pl.ds(8 * NX * h + x, 8, stride=NX)
                A[x, rows, :] = 2.0 / (1.0 + ring[turn, parity, 1, picked, :])
                C[x, rows, :] = ring[turn, parity, 0, picked, :] * (0.5 / SCALE)
        return carry

    lax.fori_loop(0, 6, load_model, 0)
    advance(0, 1)
    landed(2)
    load_states(1, raw_a)
    first_across(1)
    for n in range(1, 9):
        advance(1, n)
        if n < 8:
            advance(0, n + 1)

    def store(j, carry):
        rows = pl.ds(pl.multiple_of(8 * j, 8), 8)
        for x in range(NX):
            out[pl.ds(8 * NX * j + x, 8, stride=NX), :] = image[x, rows, :] * 0.125
        return carry

    lax.fori_loop(0, NY // 8, store, 0)

    pair.wait_send()
    cross.wait_send()

    @pl.when(away)
    def _():
        inside.wait_send()
        for b in range(2):
            forward(b).wait_send()
        for far, near in moves:
            far.wait_send()


def run_wave(blocks, model, fwd, adj, extra):
    vm = pl.BlockSpec(memory_space=pltpu.VMEM)
    anywhere = pl.BlockSpec(memory_space=pl.ANY)
    dma = pltpu.SemaphoreType.DMA
    full = lambda: pltpu.VMEM((NX, PX, NZ), jnp.float32)
    return pl.pallas_call(
        wave_kernel,
        out_shape=jax.ShapeDtypeStruct((NY * NX, NZ), jnp.float32),
        in_specs=[pl.BlockSpec(memory_space=pltpu.SMEM)] + [anywhere] * 4 + [vm] * 2,
        out_specs=vm,
        scratch_shapes=[
            *[pltpu.VMEM((NX + 8, PY, NZ), jnp.float32) for _ in range(12)],
            *[full() for _ in range(7)],
            pltpu.VMEM((2, NY * NX, NZ), jnp.float32),
            pltpu.VMEM((2, NY * NX, NZ), jnp.float32),
            pltpu.VMEM((2 * NY + 8, NZ), jnp.float32),
            pltpu.VMEM((2, 2, 2, 512, NZ), jnp.float32),
            pltpu.VMEM((3, 2, 2, 512, NZ), jnp.float32),
            pltpu.VMEM((4, 2, 2, 512, NZ), jnp.float32),
            dma((2, 2, 2)), dma((2, 2, 2)),
            dma((3,)), dma((2, 2)), dma((2,)), dma((3,)), dma((3,)), dma((3,)), dma((3,)), dma((4,)),
        ],
        compiler_params=pltpu.CompilerParams(collective_id=1, has_side_effects=True, vmem_limit_bytes=61 << 20),
        name="wave_steps",
    )(blocks, model, fwd, adj, extra, *band_pair())


def sum_kernel(blocks, partial, out, packed, ring, totals, line, ysend, yrecv, xsend, xrecv):
    xh, y, core, z, xl = position()
    meet(xh, y, core, z, xl)

    def choose(first, row, b):
        half = (2 * row + b < first).astype(jnp.int32)
        step = 8 * half + 2 * row + b - first
        inside = (step >= 0).astype(jnp.int32) * (step < 6).astype(jnp.int32)
        return half + 2 * (1 - inside), step

    def turn(d, q):
        return pltpu.make_async_remote_copy(
            src_ref=packed.at[q, d - 1], dst_ref=ring.at[q, d], send_sem=ysend.at[q, d - 1], recv_sem=yrecv.at[q, d - 1],
            device_id=device(xh, (y + d) % 4, core, z, xl), device_id_type=MESH_ID)

    def pick(target, d, q):
        first = blocks[xh * 8 + y * 2 + xl]
        for b in range(2):
            half, step = choose(first, (y + d) % 4, b)
            target[b] = partial[jnp.clip(step, 0, 5), pl.ds(CHUNK * q, CHUNK), :]

    for q in range(512 // CHUNK):
        for d in (2, 1, 3):
            pick(packed.at[q, d - 1], d, q)
            turn(d, q).start()
        pick(ring.at[q, 0], 0, q)

    def spread(k, q):
        a, b = k // 2, k % 2
        return pltpu.make_async_remote_copy(
            src_ref=totals.at[q, k], dst_ref=line.at[q, xh * 2 + xl], send_sem=xsend.at[q, k],
            recv_sem=xrecv.at[q, xh * 2 + xl], device_id=device(a, y, b, z, core), device_id_type=MESH_ID)

    def mine(k):
        return (xh == k // 2) & (core == k % 2) & (xl == core)

    for q in range(512 // CHUNK):
        for d in (1, 3, 2):
            turn(d, q).wait_recv()
        for k in range(4):
            a, b = k // 2, k % 2
            total = jnp.zeros((CHUNK, NZ), jnp.float32)
            for d in range(4):
                first = blocks[xh * 8 + ((y - d + 4) % 4) * 2 + xl]
                half, step = choose(first, y, b)
                total = total + jnp.where(jnp.full((CHUNK, NZ), half, jnp.int32) == a, ring[q, d, b], 0.0)
            totals[q, k] = total

            @pl.when(jnp.logical_not(mine(k)))
            def _():
                spread(k, q).start()

            @pl.when(mine(k))
            def _():
                line[q, xh * 2 + xl] = totals[q, k]

    for q in range(512 // CHUNK):
        for k in range(4):
            source = device(k // 2, y, xl, z, k % 2)

            @pl.when(jnp.logical_not((xh * 2 + xl == k) & (xl == core)))
            def _():
                pltpu.make_async_remote_copy(
                    src_ref=line.at[q, k], dst_ref=line.at[q, k], send_sem=xsend.at[q, k], recv_sem=xrecv.at[q, k],
                    device_id=source, device_id_type=MESH_ID).wait_recv()
        out[pl.ds(CHUNK * q, CHUNK), :] = (line[q, 0] + line[q, 1]) + (line[q, 2] + line[q, 3])

    for q in range(512 // CHUNK):
        for d in (1, 3, 2):
            turn(d, q).wait_send()
        for k in range(4):
            @pl.when(jnp.logical_not(mine(k)))
            def _():
                spread(k, q).wait_send()


def run_sum(blocks, partial):
    vm = pl.BlockSpec(memory_space=pltpu.VMEM)
    dma = pltpu.SemaphoreType.DMA
    count = 512 // CHUNK
    return pl.pallas_call(
        sum_kernel,
        out_shape=jax.ShapeDtypeStruct((512, NZ), jnp.float32),
        in_specs=[pl.BlockSpec(memory_space=pltpu.SMEM), vm],
        out_specs=vm,
        scratch_shapes=[
            pltpu.VMEM((count, 3, 2, CHUNK, NZ), jnp.float32),
            pltpu.VMEM((count, 4, 2, CHUNK, NZ), jnp.float32),
            pltpu.VMEM((count, 4, CHUNK, NZ), jnp.float32),
            pltpu.VMEM((count, 4, CHUNK, NZ), jnp.float32),
            dma((count, 3)), dma((count, 3)), dma((count, 4)), dma((count, 4)),
        ],
        compiler_params=pltpu.CompilerParams(collective_id=3, has_side_effects=True, vmem_limit_bytes=24 << 20),
        name="image_sum",
    )(blocks, partial)


def body(courant, damping, aperture_block, source_cell, receiver_depth, wavelet, receiver_data,
         forward_state, adjoint_state):
    records = receiver_data[0].reshape(2, 4, NY, NX).transpose(0, 2, 1, 3).reshape(2 * NY, NZ)
    misc = jnp.concatenate([wavelet[0], source_cell.astype(jnp.float32), receiver_depth.astype(jnp.float32),
                            jnp.zeros((NZ - 10,), jnp.float32)])
    extra = jnp.concatenate([records, jnp.broadcast_to(misc[None], (8, NZ))], axis=0)
    model = jnp.stack([courant.reshape(512, NZ), damping.reshape(512, NZ)])
    partial = run_wave(aperture_block, model, forward_state[0].reshape(2, NY * NX, NZ),
                       adjoint_state[0].reshape(2, NY * NX, NZ), extra).reshape(6, 512, NZ)
    return run_sum(aperture_block, partial).reshape(16, NX, NZ)


def solution(mesh):
    placed = (
        P("shot", "tile", None),
        P("shot", "tile", None),
        P(),
        P("shot"),
        P("shot"),
        P("shot", None),
        P("shot", None, None, "tile"),
        P("shot", None, None, "tile", None),
        P("shot", None, None, "tile", None),
    )
    return jax.shard_map(
        body, mesh=mesh, in_specs=placed, out_specs=P("shot", "tile", None), check_vma=False
    )
```

time: 218 us -> 175 us (0.80)
  Pallas kernels: 200 us -> 166 us
  local copies, waits for them, and re-layouts: 13.4 us -> 3.34 us
    pallas_call x2 -> x1, Pallas kernels: 165 us -> 130 us  [run_wave(): pl.pallas_call(wave_kernel, out_shape=jax.ShapeDtypeStruct((NY * NX, NZ),...]
    unnamed x20 -> x5, local copies, waits for them, and re-layouts: 13.4 us -> 2.11 us
where the time goes in v3:
time: 175 us; the launch traced here: 174 us
  Pallas kernels  166 us (95%)
  local copies, waits for them, and re-layouts  3.34 us (2%)
  other arithmetic  3.26 us (2%)
    pallas_call x1, Pallas kernels, run_wave(): pl.pallas_call(wave_kernel, out_shape=jax.ShapeDtypeStruct((NY * NX, NZ),...  130 us
    pallas_call x1, Pallas kernels, run_sum(): pl.pallas_call(sum_kernel, out_shape=jax.ShapeDtypeStruct((512, NZ), jnp....  35.7 us

profile of v3, /device:TPU:65, one launch (start us, length us, event | category | flops | bytes accessed | tf_op | source)
XLA Modules:
  0.0 173.6 jit_solution(10417152343542133089)
XLA Ops:
  1.3 0.7 pad_maximum_fusion.2
  2.1 1.0 copy.16
  3.1 0.1 reshape.10
  3.2 0.1 copy.14
  3.3 0.7 pad_maximum_fusion.1.extra_in
  3.9 1.9 %pad_maximum_fusion.model = f32[2,512,128]{2,1,0:T(8,128)} fusion(f32[1,512,128]{2,1,0:T(8,128)} %bitcast.18, f32[1,512,128]{2,1,0:T(8,128)} %bitcast.19), kind=kLoop, calls=%fused_computation | loop fusion | flops 131072 | bytes 1048576 | tf_op jit(solution)/shard_map/stack | solution.py:470
  5.8 0.0 copy-start.1
  5.8 129.9 %wave_steps.1 = f32[3072,128]{1,0:T(8,128)} custom-call(s32[16]{0:T(128)} %blocks.3, f32[2,512,128]{2,1,0:T(8,128)} %pad_maximum_fusion.model, f32[2,3072,128]{2,1,0:T(8,128)} %bitcast.15, f32[2,3072,128]{2,1,0:T(8,128)} %bitcast.16, f32[200,128]{1,0:T(8,128)} %pad_maximum_fusion.1.extra_in, bf16[512,256]{1,0:T(8,128)(2,1)} %constant.6.clone.band_z, ...), custom_call_target="tpu_custom_call" | custom-call | tf_op jit(solution)/shard_map/wave_steps/pallas_call | solution.py:345
  135.7 0.0 copy-done.1
  135.8 0.0 copy-start
  135.8 1.4 copy-done
  137.2 35.7 %image_sum.1 = f32[512,128]{1,0:T(8,128)S(1)} custom-call(s32[16]{0:T(128)S(1)} %copy-done.1, f32[6,512,128]{2,1,0:T(8,128)S(1)} %bitcast.13), custom_call_target="tpu_custom_call" | custom-call | tf_op jit(solution)/shard_map/image_sum/pallas_call | solution.py:447
  172.9 0.7 copy.20
  (2 shorter events, 0.0 us)
Async XLA Ops:
  5.8 129.9 %copy-start.1 = (s32[16]{0:T(128)S(1)}, s32[16]{0:T(128)}, u32[]{:S(2)}) copy-start(s32[16]{0:T(128)} %blocks.3) | copy-start | bytes 196
  135.8 1.4 copy-start

commit v4 on v3

v4 whole, which is shorter than its diff:
```python
import functools
import jax
import jax.numpy as jnp
import numpy as np
from jax import lax
from jax.experimental import pallas as pl
from jax.experimental.pallas import tpu as pltpu
from jax.sharding import PartitionSpec as P

MESH_ID = pl.DeviceIdType.MESH
SCALE = 5040.0
WEIGHTS = (-43050.0, 8064.0, -1008.0, 128.0, -9.0)
CENTRES = (-43008.0, -42.0)
NY, NX, NZ = 96, 32, 128
PY = 104
PX = 104
WIDE = 4
CHUNK = 128


def band_matrix(size, centre):
    band = centre * np.eye(size, dtype=np.float32)
    for offset in range(1, 5):
        band += WEIGHTS[offset] * (np.eye(size, k=offset) + np.eye(size, k=-offset))
    return band


def band_pair():
    deep, wide = band_matrix(NZ, CENTRES[0]), band_matrix(NY, CENTRES[1])
    deep = np.kron(np.eye(2, dtype=np.float32), deep)
    return (jnp.asarray(np.concatenate([deep, deep], axis=0), jnp.bfloat16),
            jnp.asarray(np.concatenate([wide, wide], axis=1), jnp.bfloat16))


def position():
    s = lax.axis_index("shot")
    t = lax.axis_index("tile")
    return s // 8, (s // 2) % 4, s % 2, t // 2, t % 2


def device(xh, y, core, z, xl):
    return (xh * 8 + y * 2 + core, z * 2 + xl)


def meet(xh, y, core, z, xl, more, wanted, between):
    barrier = pltpu.get_barrier_semaphore()
    peers = []
    for a in range(2):
        for b in range(2):
            for e in range(2):
                if a or b or e:
                    peers.append(device((xh + a) % 2, y, (core + b) % 2, z, (xl + e) % 2))
    for d in range(1, 4):
        peers.append(device(xh, (y + d) % 4, core, z, xl))
    for peer in peers:
        pl.semaphore_signal(barrier, inc=1, device_id=peer, device_id_type=MESH_ID)
    @pl.when(wanted)
    def _():
        pl.semaphore_signal(barrier, inc=1, device_id=more, device_id_type=MESH_ID)
    between()
    pl.semaphore_wait(barrier, len(peers) + wanted.astype(jnp.int32))


def wave_kernel(blocks, wavelet, cell_in, depth_in, courant, damping, fwd, adj, records_in, band_z, band_y, out, *scratch):
    fields = (scratch[0:6], scratch[6:12])
    Z = scratch[12:14]
    (A, C, E, T, image, raw_f, raw_a, extra_in, extra, line, packed, ring, turned, lined, ssem, rsem,
     xsend, xrecv, fsend, ysend, yrecv, msend, mrecv, local, isend, irecv, osend, orecv) = scratch[14:]
    xh, y, core, z, xl = position()
    place = 2 * z + core
    has_left = place > 0
    has_right = place < 7
    left = device(xh, y, 1 - core, z - 1 + core, xl)
    right = device(xh, y, 1 - core, z + core, xl)
    beyond = device(xh, y, 1 - core, z - 1 + 2 * core, xl)
    lane = lax.broadcasted_iota(jnp.int32, (8, NZ), 1)
    row = lax.broadcasted_iota(jnp.int32, (8, NZ), 0)

    def pack():
        for h in range(2):
            extra_in[pl.ds(NY * h, NY), :] = jnp.concatenate([records_in[4 * h + m] for m in range(4)], axis=1)
        misc = jnp.zeros((8, NZ), jnp.float32)
        for m in range(8):
            misc = jnp.where(lane == m, wavelet[0, m], misc)
        misc = jnp.where(lane == 8, cell_in[0].astype(jnp.float32), misc)
        extra_in[pl.ds(2 * NY, 8), :] = jnp.where(lane == 9, depth_in[0].astype(jnp.float32), misc)

    meet(xh, y, core, z, xl, beyond, (z - 1 + 2 * core >= 0) & (z - 1 + 2 * core < 4), pack)
    away = core != xl
    home = core == xl

    def remote(source, target, send, recv, peer):
        return pltpu.make_async_remote_copy(src_ref=source, dst_ref=target, send_sem=send, recv_sem=recv,
                                            device_id=peer, device_id_type=MESH_ID)

    model = (courant, damping)

    def own(k, peer):
        return [remote(model[a], line.at[xh, core, a], xsend.at[k, a], xrecv.at[xh, core, a], peer) for a in range(2)]

    cross = own(0, device(1 - xh, y, xl, z, 1 - xl))
    pair = own(1, device(xh, y, xl, z, 1 - xl))
    inside = own(2, device(xh, y, 1 - core, z, xl))
    keep = [pltpu.make_async_copy(model[a], line.at[xh, core, a], local.at[a]) for a in range(2)]
    for a in range(2):
        pair[a].start()
        cross[a].start()
        pl.when(away)(inside[a].start)
        pl.when(home)(keep[a].start)

    partner = device(xh, y, xl, z, core)
    moves = []
    for k, (source, target) in enumerate(((extra_in, extra), (fwd, raw_f), (adj.at[1], raw_a.at[1]), (adj.at[0], raw_a.at[0]))):
        moves.append((remote(source, target, msend.at[k], mrecv.at[k], partner),
                      pltpu.make_async_copy(source, target, local.at[2 + k])))
    for far, near in moves:
        pl.when(away)(far.start)
        pl.when(home)(near.start)

    def arrived(a, b):
        for e in range(2):
            remote(line.at[a, b, e], line.at[a, b, e], xsend.at[0, e], xrecv.at[a, b, e], partner).wait_recv()

    def forward(b):
        return [remote(line.at[xh, b, a], line.at[xh, b, a], fsend.at[b, a], xrecv.at[xh, b, a],
                       device(1 - xh, y, core, z, 1 - xl)) for a in range(2)]

    @pl.when(away)
    def _():
        for b in range(2):
            arrived(xh, b)
            for copy in forward(b):
                copy.start()

    @pl.when(home)
    def _():
        for copy in keep:
            copy.wait()
        arrived(xh, 1 - core)

    for b in range(2):
        arrived(1 - xh, b)

    def pick(target, d):
        first = blocks[xh * 8 + ((y + d) % 4) * 2 + xl]
        for b in range(2):
            half = (2 * y + b < first).astype(jnp.int32)

            def rows(i, carry):
                part = pl.ds(pl.multiple_of(64 * i, 64), 64)
                target[b, :, part, :] = line[half, b, :, part, :]
                return carry
            lax.fori_loop(0, 8, rows, 0)

    def round_trip(d):
        return remote(packed.at[d - 1], ring.at[d], ysend.at[d - 1], yrecv.at[d - 1],
                      device(xh, (y + d) % 4, core, z, xl))

    for d in (2, 1, 3):
        pick(packed.at[d - 1], d)
        round_trip(d).start()
    def landed(i):
        far, near = moves[i]
        pl.when(away)(far.wait_recv)
        pl.when(home)(near.wait)

    def halo(f, slot, par, side):
        if side == 0:
            return pltpu.make_async_remote_copy(
                src_ref=fields[f][slot].at[pl.ds(4, 4), pl.ds(0, NY), :],
                dst_ref=fields[f][slot].at[pl.ds(36, 4), pl.ds(0, NY), :],
                send_sem=ssem.at[f, 0, par], recv_sem=rsem.at[f, 0, par],
                device_id=left, device_id_type=MESH_ID)
        return pltpu.make_async_remote_copy(
            src_ref=fields[f][slot].at[pl.ds(32, 4), pl.ds(0, NY), :],
            dst_ref=fields[f][slot].at[pl.ds(0, 4), pl.ds(0, NY), :],
            send_sem=ssem.at[f, 1, par], recv_sem=rsem.at[f, 1, par],
            device_id=right, device_id_type=MESH_ID)

    def send(f, slot, par, side):
        @pl.when(has_left if side == 0 else has_right)
        def _():
            halo(f, slot, par, side).start()

    def wait(f, slot, par):
        @pl.when(has_left)
        def _():
            halo(f, slot, par, 0).wait_send()
            halo(f, slot, par, 1).wait_recv()

        @pl.when(has_right)
        def _():
            halo(f, slot, par, 1).wait_send()
            halo(f, slot, par, 0).wait_recv()

    zero_side = jnp.zeros((4, NY, NZ), jnp.float32)

    @pl.when(place == 0)
    def _():
        for f in range(2):
            for slot in range(6):
                fields[f][slot][pl.ds(0, 4), pl.ds(0, NY), :] = zero_side

    @pl.when(place == 7)
    def _():
        for f in range(2):
            for slot in range(6):
                fields[f][slot][pl.ds(36, 4), pl.ds(0, NY), :] = zero_side

    landed(0)
    depth = jnp.broadcast_to(extra[pl.ds(192, 8), pl.ds(9, 1)], (8, NZ))
    plane = jnp.where(lane.astype(jnp.float32) == depth, 0.5, 0.0)
    cell = jnp.broadcast_to(extra[pl.ds(192, 8), pl.ds(8, 1)], (8, NZ))
    turns = [(depth + m) - jnp.where(depth + m >= NZ, float(NZ), 0.0) for m in range(8)]

    def load_extra(j, carry):
        rows = pl.ds(pl.multiple_of(8 * j, 8), 8)
        records = [extra[pl.ds(pl.multiple_of(NY * h + 8 * j, 8), 8), :] for h in range(2)]
        for x in range(NX):
            placed = jnp.zeros((8, NZ), jnp.float32)
            for m in range(8):
                at = (m % 4) * NX + x
                value = jnp.broadcast_to(records[m // 4][:, at:at + 1], (8, NZ))
                placed = jnp.where(lane.astype(jnp.float32) == turns[m], value, placed)
            T[x, rows, :] = placed
            index = (place * NX + x) * (NY * NZ) + (row + 8 * j) * NZ + lane
            E[x, rows, :] = jnp.where(index.astype(jnp.float32) == cell, 0.5, 0.0)
        return carry

    lax.fori_loop(0, NY // 8, load_extra, 0)

    def clear(x, carry):
        image[x] = jnp.zeros((6, 16, NZ), jnp.float32)
        return carry

    lax.fori_loop(0, NX, clear, 0)

    def load_state(f, slot, source):
        def planes(picks):
            def tiles(j, carry):
                rows = pl.ds(pl.multiple_of(8 * j, 8), 8)
                for x in picks:
                    fields[f][slot][4 + x, rows, :] = source[pl.ds(8 * NX * j + x, 8, stride=NX), :]
                return carry
            lax.fori_loop(0, NY // 8, tiles, 0)

        planes([*range(4), *range(28, 32)])
        if slot == 1:
            send(f, 1, 0, 0)
            send(f, 1, 0, 1)
        planes(range(4, 28))

    def across(f, slot, x):
        for h in range(0, WIDE, 2):
            u = fields[f][slot][pl.ds(4 + x + h, 2), pl.ds(0, NY), :]
            high = u.astype(jnp.bfloat16)
            low = (u - high.astype(jnp.float32)).astype(jnp.bfloat16)
            high = jnp.concatenate([high[0], high[1]], axis=1)
            low = jnp.concatenate([low[0], low[1]], axis=1)
            rows = jnp.concatenate([high, low, band_y[...]], axis=1)
            columns = jnp.concatenate([band_z[...], high, low], axis=0)
            both = jnp.dot(rows, columns, preferred_element_type=jnp.float32)
            Z[f][x + h, pl.ds(0, NY), :] = both[:, :NZ]
            Z[f][x + h + 1, pl.ds(0, NY), :] = both[:, NZ:]

    def slot_of(n):
        return n + 1 if n < 5 else (n + 1) % 2

    def advance(f, n):
        cur, prev, new = fields[f][slot_of(n - 1)], fields[f][slot_of(n - 2)], fields[f][slot_of(n)]
        other = fields[1 - f][slot_of(9 - n)] if n > 4 else None
        late = f == 1 and n == 1
        if not late:
            wait(f, slot_of(n - 1), (n - 1) % 2)
        amp = jnp.broadcast_to(extra[pl.ds(192, 8), pl.ds(n - 1, 1)], (8, NZ))

        def planes(i, carry):
            x = WIDE * i
            if f == 0 and n > 1:
                across(1, slot_of(n - 1), x)
            if f == 1 and n < 8:
                across(0, slot_of(n), x)
            for j in range(NY // 8):
                rows = pl.ds(8 * j, 8)
                wide = cur[pl.ds(x, WIDE + 8), rows, :]
                u = wide[4:4 + WIDE]
                acc = Z[f][pl.ds(x, WIDE), rows, :]
                for k in range(1, 5):
                    acc = acc + WEIGHTS[k] * (wide[4 + k:4 + k + WIDE] + wide[4 - k:4 - k + WIDE])
                v = prev[pl.ds(4 + x, WIDE), rows, :]
                if f == 0:
                    force = E[pl.ds(x, WIDE), rows, :] * amp[None]
                else:
                    force = jnp.stack([pltpu.roll(T[x + h, rows, :], NZ - (8 - n), 1) * plane for h in range(WIDE)])
                w = v + A[pl.ds(x, WIDE), rows, :] * ((u - v) + (C[pl.ds(x, WIDE), rows, :] * acc + force))
                new[pl.ds(4 + x, WIDE), rows, :] = w
                if other is not None:
                    image[pl.ds(x, WIDE), j // 2, pl.ds(8 * (j % 2), 8), :] += w * other[pl.ds(4 + x, WIDE), rows, :]
            return carry

        parts = [(0, 4 // WIDE, 0), (28 // WIDE, 32 // WIDE, 1), (4 // WIDE, 28 // WIDE, None)]
        for first, last, side in (parts[2:] + parts[:2] if late else parts):
            if late and side == 0:
                wait(f, slot_of(n - 1), (n - 1) % 2)
            lax.fori_loop(first, last, planes, 0)
            if side is not None and n < 8:
                send(f, slot_of(n), n % 2, side)

    def first_across(f):
        def planes(i, carry):
            across(f, 1, WIDE * i)
            return carry
        lax.fori_loop(0, NX // WIDE, planes, 0)

    landed(1)
    load_state(0, 1, raw_f.at[0])
    load_state(0, 0, raw_f.at[1])
    first_across(0)
    pick(ring.at[0], 0)
    for d in (1, 3, 2):
        round_trip(d).wait()


    first = blocks[xh * 8 + y * 2 + xl]

    def load_model(k, carry):
        j = first + k
        turn = (y - (j // 2) % 4 + 4) % 4
        parity = j % 2
        for h in range(2):
            rows = pl.ds(pl.multiple_of(16 * k + 8 * h, 8), 8)
            for x in range(NX):
                picked = pl.ds(8 * NX * h + x, 8, stride=NX)
                A[x, rows, :] = 2.0 / (1.0 + ring[turn, parity, 1, picked, :])
                C[x, rows, :] = ring[turn, parity, 0, picked, :] * (0.5 / SCALE)
        return carry

    lax.fori_loop(0, 6, load_model, 0)
    advance(0, 1)
    landed(2)
    load_state(1, 0, raw_a.at[1])
    landed(3)
    load_state(1, 1, raw_a.at[0])
    first_across(1)
    for n in range(1, 9):
        advance(1, n)
        if n < 8:
            advance(0, n + 1)

    def choose(first, row, b):
        half = (2 * row + b < first).astype(jnp.int32)
        step = 8 * half + 2 * row + b - first
        inside = (step >= 0).astype(jnp.int32) * (step < 6).astype(jnp.int32)
        return half + 2 * (1 - inside), step

    def packet(d, q):
        return raw_f.at[0, pl.ds(256 * (3 * q + d - 1), 256), :]

    def total_of(k, q):
        return raw_f.at[1, pl.ds(CHUNK * (4 * q + k), CHUNK), :]

    def turn(d, q):
        return remote(packet(d, q), turned.at[q, d], isend.at[q, d - 1], irecv.at[q, d - 1],
                      device(xh, (y + d) % 4, core, z, xl))

    def pick_image(target, d, q):
        for b in range(2):
            half, step = choose(first, (y + d) % 4, b)
            value = image[pl.ds(8 * q, 8), jnp.clip(step, 0, 5), :, :] * 0.125
            target[pl.ds(CHUNK * b, CHUNK), :] = value.reshape(CHUNK, NZ)

    for q in range(4):
        for d in (2, 1, 3):
            pick_image(packet(d, q), d, q)
            turn(d, q).start()
        pick_image(turned.at[q, 0], 0, q)

    def spread(k, q):
        return remote(total_of(k, q), lined.at[q, xh * 2 + xl], osend.at[q, k], orecv.at[q, xh * 2 + xl],
                      device(k // 2, y, k % 2, z, core))

    def mine(k):
        return (xh == k // 2) & (core == k % 2) & (xl == core)

    for q in range(4):
        for d in (1, 3, 2):
            turn(d, q).wait_recv()
        for k in range(4):
            a, b = k // 2, k % 2
            total = jnp.zeros((CHUNK, NZ), jnp.float32)
            for d in range(4):
                half, step = choose(blocks[xh * 8 + ((y - d + 4) % 4) * 2 + xl], y, b)
                part = turned[q, d, pl.ds(CHUNK * b, CHUNK), :]
                total = total + jnp.where(jnp.full((CHUNK, NZ), half, jnp.int32) == a, part, 0.0)
            total_of(k, q)[...] = total

            @pl.when(jnp.logical_not(mine(k)))
            def _():
                spread(k, q).start()

            @pl.when(mine(k))
            def _():
                lined[q, xh * 2 + xl] = total_of(k, q)[...]

    for q in range(4):
        for k in range(4):
            @pl.when(jnp.logical_not((xh * 2 + xl == k) & (xl == core)))
            def _():
                remote(lined.at[q, k], lined.at[q, k], osend.at[q, k], orecv.at[q, k],
                       device(k // 2, y, xl, z, k % 2)).wait_recv()
        total = (lined[q, 0] + lined[q, 1]) + (lined[q, 2] + lined[q, 3])
        for i in range(8):
            for h in range(2):
                out[pl.ds(8 * NX * h + 8 * q + i, 8, stride=NX), :] = total[16 * i + 8 * h:16 * i + 8 * h + 8]

    for q in range(4):
        for d in (1, 3, 2):
            turn(d, q).wait_send()
        for k in range(4):
            @pl.when(jnp.logical_not(mine(k)))
            def _():
                spread(k, q).wait_send()

    for copy in pair + cross:
        copy.wait_send()

    @pl.when(away)
    def _():
        for copy in inside + forward(0) + forward(1):
            copy.wait_send()
        for far, near in moves:
            far.wait_send()


def run_wave(blocks, wavelet, cell, depth, courant, damping, fwd, adj, records):
    vm = pl.BlockSpec(memory_space=pltpu.VMEM)
    scalars = pl.BlockSpec(memory_space=pltpu.SMEM)
    anywhere = pl.BlockSpec(memory_space=pl.ANY)
    dma = pltpu.SemaphoreType.DMA
    full = lambda: pltpu.VMEM((NX, PX, NZ), jnp.float32)
    flat = lambda *shape: pltpu.VMEM((*shape, NZ), jnp.float32)
    return pl.pallas_call(
        wave_kernel,
        out_shape=jax.ShapeDtypeStruct((512, NZ), jnp.float32),
        in_specs=[scalars] * 4 + [anywhere] * 4 + [vm] * 3,
        out_specs=vm,
        scratch_shapes=[
            *[flat(NX + 8, PY) for _ in range(12)],
            *[full() for _ in range(6)],
            flat(NX, 6, 16),
            flat(2, NY * NX),
            flat(2, NY * NX),
            flat(2 * NY + 8),
            flat(2 * NY + 8),
            flat(2, 2, 2, 512),
            flat(3, 2, 2, 512),
            flat(4, 2, 2, 512),
            flat(4, 4, 256),
            flat(4, 4, CHUNK),
            dma((2, 2, 2)), dma((2, 2, 2)),
            dma((3, 2)), dma((2, 2, 2)), dma((2, 2)), dma((3,)), dma((3,)), dma((4,)), dma((4,)), dma((6,)),
            dma((4, 3)), dma((4, 3)), dma((4, 4)), dma((4, 4)),
        ],
        compiler_params=pltpu.CompilerParams(collective_id=1, has_side_effects=True, vmem_limit_bytes=61 << 20),
        name="wave_steps",
    )(blocks, wavelet, cell, depth, courant, damping, fwd, adj, records, *band_pair())


def body(courant, damping, aperture_block, source_cell, receiver_depth, wavelet, receiver_data,
         forward_state, adjoint_state):
    image = run_wave(aperture_block, wavelet, source_cell, receiver_depth, courant.reshape(512, NZ),
                     damping.reshape(512, NZ), forward_state[0].reshape(2, NY * NX, NZ),
                     adjoint_state[0].reshape(2, NY * NX, NZ), receiver_data[0])
    return image.reshape(16, NX, NZ)


def solution(mesh):
    placed = (
        P("shot", "tile", None),
        P("shot", "tile", None),
        P(),
        P("shot"),
        P("shot"),
        P("shot", None),
        P("shot", None, None, "tile"),
        P("shot", None, None, "tile", None),
        P("shot", None, None, "tile", None),
    )
    return jax.shard_map(
        body, mesh=mesh, in_specs=placed, out_specs=P("shot", "tile", None), check_vma=False
    )
```

time: 175 us -> 165 us (0.943)
  Pallas kernels: 166 us -> 160 us
  other arithmetic: 3.26 us -> 0 us
    pallas_call x2 -> x1, Pallas kernels: 166 us -> 160 us  [run_wave(): pl.pallas_call(wave_kernel, out_shape=jax.ShapeDtypeStruct((512, NZ), jnp...]
    another operation x1 -> x0, other arithmetic: 1.86 us -> none  [body(): model = jnp.stack([courant.reshape(512, NZ), damping.reshape(512, NZ)])]
where the time goes in v4:
time: 165 us
  Pallas kernels  160 us (97%)
  local copies, waits for them, and re-layouts  3.49 us (2%)
    pallas_call x1, Pallas kernels, run_wave(): pl.pallas_call(wave_kernel, out_shape=jax.ShapeDtypeStruct((512, NZ), jnp...  160 us
    unnamed x2, local copies, waits for them, and re-layouts  3.49 us

profile of v4, /device:TPU:65, one launch (start us, length us, event | category | flops | bytes accessed | tf_op | source)
XLA Modules:
  0.0 164.8 jit_solution(2958686296345717993)
XLA Ops:
  1.3 1.8 %copy.12 = f32[1,8,96,32]{3,2,1,0:T(8,128)} copy(f32[1,8,96,32]{2,3,1,0:T(8,128)} %param.17) | data formatting | bytes 196608 | tf_op args[6]
  3.1 160.0 %wave_steps.1 = f32[512,128]{1,0:T(8,128)} custom-call(s32[16]{0:T(128)} %blocks.1, f32[1,8]{1,0:T(1,128)} %wavelet.1, s32[1]{0:T(128)S(6)} %copy.14.cell_in, s32[1]{0:T(128)S(6)} %copy.15.depth_in, f32[512,128]{1,0:T(8,128)} %bitcast.10, f32[512,128]{1,0:T(8,128)} %bitcast.11, f32[2,3072,128]{2,1,0:T(8,128)} %bitcast.6, f32[2,3072,128]{2,1,0:T(8,128)} %bitcast.7, ...), custom_call_target="tpu_custom_call" | custom-call | tf_op jit(solution)/shard_map/wave_steps/pallas_call | solution.py:442
  163.1 1.7 %copy.16 = f32[16,32,128]{2,1,0:T(8,128)} copy(f32[16,32,128]{2,1,0:T(8,128)} %bitcast.9) | data formatting | bytes 524288

commit v5 on v4

--- a/solution.py
+++ b/solution.py
@@ -15,7 +15,8 @@
 PY = 104
 PX = 104
 WIDE = 4
-CHUNK = 128
+PARTS = 8
+CHUNK = 512 // PARTS
 
 
 def band_matrix(size, centre):
@@ -78,7 +79,7 @@
 
     def pack():
         for h in range(2):
-            extra_in[pl.ds(NY * h, NY), :] = jnp.concatenate([records_in[4 * h + m] for m in range(4)], axis=1)
+            extra_in[pl.ds(NY * h, NY), :] = records_in[pl.ds(4 * h, 4)].reshape(4 * NX, NY).T
         misc = jnp.zeros((8, NZ), jnp.float32)
         for m in range(8):
             misc = jnp.where(lane == m, wavelet[0, m], misc)
@@ -110,7 +111,7 @@
 
     partner = device(xh, y, xl, z, core)
     moves = []
-    for k, (source, target) in enumerate(((extra_in, extra), (fwd, raw_f), (adj.at[1], raw_a.at[1]), (adj.at[0], raw_a.at[0]))):
+    for k, (source, target) in enumerate(((extra_in, extra), (fwd, raw_f), (adj.at[0], raw_a.at[0]), (adj.at[1], raw_a.at[1]))):
         moves.append((remote(source, target, msend.at[k], mrecv.at[k], partner),
                       pltpu.make_async_copy(source, target, local.at[2 + k])))
     for far, near in moves:
@@ -250,6 +251,36 @@
             send(f, 1, 0, 1)
         planes(range(4, 28))
 
+    first = blocks[xh * 8 + y * 2 + xl]
+
+    def choose(first, row, b):
+        half = (2 * row + b < first).astype(jnp.int32)
+        step = 8 * half + 2 * row + b - first
+        inside = (step >= 0).astype(jnp.int32) * (step < 6).astype(jnp.int32)
+        return half + 2 * (1 - inside), step
+
+    def packet(d, q):
+        return raw_f.at[0, pl.ds(2 * CHUNK * (3 * q + d - 1), 2 * CHUNK), :]
+
+    def total_of(k, q):
+        return raw_f.at[1, pl.ds(CHUNK * (4 * q + k), CHUNK), :]
+
+    def turn(d, q):
+        return remote(packet(d, q), turned.at[q, d], isend.at[q, d - 1], irecv.at[q, d - 1],
+                      device(xh, (y + d) % 4, core, z, xl))
+
+    def pick_image(target, d, q):
+        for b in range(2):
+            half, step = choose(first, (y + d) % 4, b)
+            value = image[pl.ds(NX // PARTS * q, NX // PARTS), jnp.clip(step, 0, 5), :, :] * 0.125
+            target[pl.ds(CHUNK * b, CHUNK), :] = value.reshape(CHUNK, NZ)
+
+    def send_image(q):
+        for d in (2, 1, 3):
+            pick_image(packet(d, q), d, q)
+            turn(d, q).start()
+        pick_image(turned.at[q, 0], 0, q)
+
     def across(f, slot, x):
         for h in range(0, WIDE, 2):
             u = fields[f][slot][pl.ds(4 + x + h, 2), pl.ds(0, NY), :]
@@ -269,9 +300,7 @@
     def advance(f, n):
         cur, prev, new = fields[f][slot_of(n - 1)], fields[f][slot_of(n - 2)], fields[f][slot_of(n)]
         other = fields[1 - f][slot_of(9 - n)] if n > 4 else None
-        late = f == 1 and n == 1
-        if not late:
-            wait(f, slot_of(n - 1), (n - 1) % 2)
+        wait(f, slot_of(n - 1), (n - 1) % 2)
         amp = jnp.broadcast_to(extra[pl.ds(192, 8), pl.ds(n - 1, 1)], (8, NZ))
 
         def planes(i, carry):
@@ -298,10 +327,13 @@
                     image[pl.ds(x, WIDE), j // 2, pl.ds(8 * (j % 2), 8), :] += w * other[pl.ds(4 + x, WIDE), rows, :]
             return carry
 
+        if f == 1 and n == 8:
+            for i in range(PARTS):
+                planes(i, 0)
+                send_image(i)
+            return
         parts = [(0, 4 // WIDE, 0), (28 // WIDE, 32 // WIDE, 1), (4 // WIDE, 28 // WIDE, None)]
-        for first, last, side in (parts[2:] + parts[:2] if late else parts):
-            if late and side == 0:
-                wait(f, slot_of(n - 1), (n - 1) % 2)
+        for first, last, side in parts:
             lax.fori_loop(first, last, planes, 0)
             if side is not None and n < 8:
                 send(f, slot_of(n), n % 2, side)
@@ -320,8 +352,6 @@
     for d in (1, 3, 2):
         round_trip(d).wait()
 
-
-    first = blocks[xh * 8 + y * 2 + xl]
 
     def load_model(k, carry):
         j = first + k
@@ -338,43 +368,15 @@
     lax.fori_loop(0, 6, load_model, 0)
     advance(0, 1)
     landed(2)
-    load_state(1, 0, raw_a.at[1])
-    landed(3)
     load_state(1, 1, raw_a.at[0])
     first_across(1)
+    landed(3)
+    load_state(1, 0, raw_a.at[1])
     for n in range(1, 9):
         advance(1, n)
         if n < 8:
             advance(0, n + 1)
 
-    def choose(first, row, b):
-        half = (2 * row + b < first).astype(jnp.int32)
-        step = 8 * half + 2 * row + b - first
-        inside = (step >= 0).astype(jnp.int32) * (step < 6).astype(jnp.int32)
-        return half + 2 * (1 - inside), step
-
-    def packet(d, q):
-        return raw_f.at[0, pl.ds(256 * (3 * q + d - 1), 256), :]
-
-    def total_of(k, q):
-        return raw_f.at[1, pl.ds(CHUNK * (4 * q + k), CHUNK), :]
-
-    def turn(d, q):
-        return remote(packet(d, q), turned.at[q, d], isend.at[q, d - 1], irecv.at[q, d - 1],
-                      device(xh, (y + d) % 4, core, z, xl))
-
-    def pick_image(target, d, q):
-        for b in range(2):
-            half, step = choose(first, (y + d) % 4, b)
-            value = image[pl.ds(8 * q, 8), jnp.clip(step, 0, 5), :, :] * 0.125
-            target[pl.ds(CHUNK * b, CHUNK), :] = value.reshape(CHUNK, NZ)
-
-    for q in range(4):
-        for d in (2, 1, 3):
-            pick_image(packet(d, q), d, q)
-            turn(d, q).start()
-        pick_image(turned.at[q, 0], 0, q)
-
     def spread(k, q):
         return remote(total_of(k, q), lined.at[q, xh * 2 + xl], osend.at[q, k], orecv.at[q, xh * 2 + xl],
                       device(k // 2, y, k % 2, z, core))
@@ -382,7 +384,7 @@
     def mine(k):
         return (xh == k // 2) & (core == k % 2) & (xl == core)
 
-    for q in range(4):
+    for q in range(PARTS):
         for d in (1, 3, 2):
             turn(d, q).wait_recv()
         for k in range(4):
@@ -402,18 +404,18 @@
             def _():
                 lined[q, xh * 2 + xl] = total_of(k, q)[...]
 
-    for q in range(4):
+    for q in range(PARTS):
         for k in range(4):
             @pl.when(jnp.logical_not((xh * 2 + xl == k) & (xl == core)))
             def _():
                 remote(lined.at[q, k], lined.at[q, k], osend.at[q, k], orecv.at[q, k],
                        device(k // 2, y, xl, z, k % 2)).wait_recv()
         total = (lined[q, 0] + lined[q, 1]) + (lined[q, 2] + lined[q, 3])
-        for i in range(8):
+        for i in range(NX // PARTS):
             for h in range(2):
-                out[pl.ds(8 * NX * h + 8 * q + i, 8, stride=NX), :] = total[16 * i + 8 * h:16 * i + 8 * h + 8]
-
-    for q in range(4):
+                out[pl.ds(8 * NX * h + NX // PARTS * q + i, 8, stride=NX), :] = total[16 * i + 8 * h:16 * i + 8 * h + 8]
+
+    for q in range(PARTS):
         for d in (1, 3, 2):
             turn(d, q).wait_send()
         for k in range(4):
@@ -455,11 +457,11 @@
             flat(2, 2, 2, 512),
             flat(3, 2, 2, 512),
             flat(4, 2, 2, 512),
-            flat(4, 4, 256),
-            flat(4, 4, CHUNK),
+            flat(PARTS, 4, 2 * CHUNK),
+            flat(PARTS, 4, CHUNK),
             dma((2, 2, 2)), dma((2, 2, 2)),
             dma((3, 2)), dma((2, 2, 2)), dma((2, 2)), dma((3,)), dma((3,)), dma((4,)), dma((4,)), dma((6,)),
-            dma((4, 3)), dma((4, 3)), dma((4, 4)), dma((4, 4)),
+            dma((PARTS, 3)), dma((PARTS, 3)), dma((PARTS, 4)), dma((PARTS, 4)),
         ],
         compiler_params=pltpu.CompilerParams(collective_id=1, has_side_effects=True, vmem_limit_bytes=61 << 20),
         name="wave_steps",
@@ -470,7 +472,7 @@
          forward_state, adjoint_state):
     image = run_wave(aperture_block, wavelet, source_cell, receiver_depth, courant.reshape(512, NZ),
                      damping.reshape(512, NZ), forward_state[0].reshape(2, NY * NX, NZ),
-                     adjoint_state[0].reshape(2, NY * NX, NZ), receiver_data[0])
+                     adjoint_state[0].reshape(2, NY * NX, NZ), receiver_data[0].transpose(0, 2, 1))
     return image.reshape(16, NX, NZ)
 
 

time: 165 us -> 158 us (0.958)
  Pallas kernels: 160 us -> 155 us
  local copies, waits for them, and re-layouts: 3.49 us -> 1.67 us
    pallas_call x1, Pallas kernels: 160 us -> 155 us  [run_wave(): pl.pallas_call(wave_kernel, out_shape=jax.ShapeDtypeStruct((512, NZ), jnp...]
    unnamed x2 -> x1, local copies, waits for them, and re-layouts: 3.49 us -> 1.67 us
where the time goes in v5:
time: 158 us
  Pallas kernels  155 us (98%)
  local copies, waits for them, and re-layouts  1.67 us (1%)
    pallas_call x1, Pallas kernels, run_wave(): pl.pallas_call(wave_kernel, out_shape=jax.ShapeDtypeStruct((512, NZ), jnp...  155 us

profile of v5, /device:TPU:65, one launch (start us, length us, event | category | flops | bytes accessed | tf_op | source)
XLA Modules:
  0.0 157.7 jit_solution(15631113497917625224)
XLA Ops:
  1.3 154.7 %wave_steps.1 = f32[512,128]{1,0:T(8,128)} custom-call(s32[16]{0:T(128)} %blocks.1, f32[1,8]{1,0:T(1,128)} %wavelet.1, s32[1]{0:T(128)S(6)} %copy.13.cell_in, s32[1]{0:T(128)S(6)} %copy.14.depth_in, f32[512,128]{1,0:T(8,128)} %bitcast.11, f32[512,128]{1,0:T(8,128)} %bitcast.12, f32[2,3072,128]{2,1,0:T(8,128)} %bitcast.8, f32[2,3072,128]{2,1,0:T(8,128)} %bitcast.9, ...), custom_call_target="tpu_custom_call" | custom-call | tf_op jit(solution)/shard_map/wave_steps/pallas_call | solution.py:444
  156.0 1.7 %copy.15 = f32[16,32,128]{2,1,0:T(8,128)} copy(f32[16,32,128]{2,1,0:T(8,128)} %bitcast.10) | data formatting | bytes 524288

commit v6 on v5

--- a/solution.py
+++ b/solution.py
@@ -66,7 +66,8 @@
     fields = (scratch[0:6], scratch[6:12])
     Z = scratch[12:14]
     (A, C, E, T, image, raw_f, raw_a, extra_in, extra, line, packed, ring, turned, lined, ssem, rsem,
-     xsend, xrecv, fsend, ysend, yrecv, msend, mrecv, local, isend, irecv, osend, orecv) = scratch[14:]
+     xsend, xrecv, fsend, ysend, yrecv, msend, mrecv, local, isend, irecv, osend, orecv, xfirst, ysecond,
+     csend, crecv, dsend, drecv) = scratch[14:]
     xh, y, core, z, xl = position()
     place = 2 * z + core
     has_left = place > 0
@@ -280,6 +281,35 @@
             pick_image(packet(d, q), d, q)
             turn(d, q).start()
         pick_image(turned.at[q, 0], 0, q)
+
+    def mine(k):
+        return (xh == k // 2) & (core == k % 2) & (xl == core)
+
+    def line_copy(k):
+        return remote(raw_a.at[0, pl.ds(4 * CHUNK * k, 4 * CHUNK), :], xfirst.at[xh * 2 + xl], csend.at[k],
+                      crecv.at[xh * 2 + xl], device(k // 2, y, k % 2, z, core))
+
+    def send_first():
+        for k in range(4):
+            for r in range(4):
+                step = 8 * (k // 2) + 2 * r + k % 2 - first
+                inside = (step >= 0).astype(jnp.int32) * (step < 6).astype(jnp.int32)
+                value = image[pl.ds(0, NX // PARTS), jnp.clip(step, 0, 5), :, :] * 0.125
+                kept = jnp.full((CHUNK, NZ), inside, jnp.int32) == 1
+                raw_a[0, pl.ds(CHUNK * (4 * k + r), CHUNK), :] = jnp.where(kept, value.reshape(CHUNK, NZ), 0.0)
+
+            @pl.when(jnp.logical_not(mine(k)))
+            def _():
+                line_copy(k).start()
+
+            @pl.when(mine(k))
+            def _():
+                xfirst[xh * 2 + xl] = raw_a[0, pl.ds(4 * CHUNK * k, 4 * CHUNK), :]
+
+    def column_copy(d):
+        row = (y + d) % 4
+        return remote(raw_a.at[1, pl.ds(pl.multiple_of(CHUNK * row, CHUNK), CHUNK), :], ysecond.at[d], dsend.at[d - 1],
+                      drecv.at[d - 1], device(xh, row, core, z, xl))
 
     def across(f, slot, x):
         for h in range(0, WIDE, 2):
@@ -330,7 +360,10 @@
         if f == 1 and n == 8:
             for i in range(PARTS):
                 planes(i, 0)
-                send_image(i)
+                if i == 0:
+                    send_first()
+                else:
+                    send_image(i)
             return
         parts = [(0, 4 // WIDE, 0), (28 // WIDE, 32 // WIDE, 1), (4 // WIDE, 28 // WIDE, None)]
         for first, last, side in parts:
@@ -381,10 +414,16 @@
         return remote(total_of(k, q), lined.at[q, xh * 2 + xl], osend.at[q, k], orecv.at[q, xh * 2 + xl],
                       device(k // 2, y, k % 2, z, core))
 
-    def mine(k):
-        return (xh == k // 2) & (core == k % 2) & (xl == core)
-
-    for q in range(PARTS):
+    for k in range(4):
+        @pl.when(jnp.logical_not((xh * 2 + xl == k) & (xl == core)))
+        def _():
+            remote(xfirst.at[k], xfirst.at[k], csend.at[0], crecv.at[k], device(k // 2, y, xl, z, k % 2)).wait_recv()
+    raw_a[1, pl.ds(0, 4 * CHUNK), :] = (xfirst[0] + xfirst[1]) + (xfirst[2] + xfirst[3])
+    for d in (2, 1, 3):
+        column_copy(d).start()
+    ysecond[0] = raw_a[1, pl.ds(pl.multiple_of(CHUNK * y, CHUNK), CHUNK), :]
+
+    for q in range(1, PARTS):
         for d in (1, 3, 2):
             turn(d, q).wait_recv()
         for k in range(4):
@@ -405,17 +444,28 @@
                 lined[q, xh * 2 + xl] = total_of(k, q)[...]
 
     for q in range(PARTS):
-        for k in range(4):
-            @pl.when(jnp.logical_not((xh * 2 + xl == k) & (xl == core)))
-            def _():
-                remote(lined.at[q, k], lined.at[q, k], osend.at[q, k], orecv.at[q, k],
-                       device(k // 2, y, xl, z, k % 2)).wait_recv()
-        total = (lined[q, 0] + lined[q, 1]) + (lined[q, 2] + lined[q, 3])
+        if q == 0:
+            for d in (1, 3, 2):
+                column_copy(d).wait_recv()
+            total = (ysecond[0] + ysecond[1]) + (ysecond[2] + ysecond[3])
+        else:
+            for k in range(4):
+                @pl.when(jnp.logical_not((xh * 2 + xl == k) & (xl == core)))
+                def _():
+                    remote(lined.at[q, k], lined.at[q, k], osend.at[q, k], orecv.at[q, k],
+                           device(k // 2, y, xl, z, k % 2)).wait_recv()
+            total = (lined[q, 0] + lined[q, 1]) + (lined[q, 2] + lined[q, 3])
         for i in range(NX // PARTS):
             for h in range(2):
                 out[pl.ds(8 * NX * h + NX // PARTS * q + i, 8, stride=NX), :] = total[16 * i + 8 * h:16 * i + 8 * h + 8]
 
-    for q in range(PARTS):
+    for d in (1, 3, 2):
+        column_copy(d).wait_send()
+    for k in range(4):
+        @pl.when(jnp.logical_not(mine(k)))
+        def _():
+            line_copy(k).wait_send()
+    for q in range(1, PARTS):
         for d in (1, 3, 2):
             turn(d, q).wait_send()
         for k in range(4):
@@ -462,6 +512,9 @@
             dma((2, 2, 2)), dma((2, 2, 2)),
             dma((3, 2)), dma((2, 2, 2)), dma((2, 2)), dma((3,)), dma((3,)), dma((4,)), dma((4,)), dma((6,)),
             dma((PARTS, 3)), dma((PARTS, 3)), dma((PARTS, 4)), dma((PARTS, 4)),
+            flat(4, 4 * CHUNK),
+            flat(4, CHUNK),
+            dma((4,)), dma((4,)), dma((3,)), dma((3,)),
         ],
         compiler_params=pltpu.CompilerParams(collective_id=1, has_side_effects=True, vmem_limit_bytes=61 << 20),
         name="wave_steps",

time: 158 us -> 156 us (0.987)
  Pallas kernels: 155 us -> 153 us
    pallas_call x1, Pallas kernels: 155 us -> 153 us  [run_wave(): pl.pallas_call(wave_kernel, out_shape=jax.ShapeDtypeStruct((512, NZ), jnp...]
where the time goes in v6:
time: 156 us
  Pallas kernels  153 us (98%)
  local copies, waits for them, and re-layouts  1.67 us (1%)
    pallas_call x1, Pallas kernels, run_wave(): pl.pallas_call(wave_kernel, out_shape=jax.ShapeDtypeStruct((512, NZ), jnp...  153 us

profile of v6, /device:TPU:65, one launch (start us, length us, event | category | flops | bytes accessed | tf_op | source)
XLA Modules:
  0.0 155.7 jit_solution(9426350083441071236)
XLA Ops:
  1.3 152.7 %wave_steps.1 = f32[512,128]{1,0:T(8,128)} custom-call(s32[16]{0:T(128)} %blocks.1, f32[1,8]{1,0:T(1,128)} %wavelet.1, s32[1]{0:T(128)S(6)} %copy.13.cell_in, s32[1]{0:T(128)S(6)} %copy.14.depth_in, f32[512,128]{1,0:T(8,128)} %bitcast.11, f32[512,128]{1,0:T(8,128)} %bitcast.12, f32[2,3072,128]{2,1,0:T(8,128)} %bitcast.8, f32[2,3072,128]{2,1,0:T(8,128)} %bitcast.9, ...), custom_call_target="tpu_custom_call" | custom-call | tf_op jit(solution)/shard_map/wave_steps/pallas_call | solution.py:494
  154.0 1.7 %copy.15 = f32[16,32,128]{2,1,0:T(8,128)} copy(f32[16,32,128]{2,1,0:T(8,128)} %bitcast.10) | data formatting | bytes 524288

commit v7 on v6

--- a/solution.py
+++ b/solution.py
@@ -15,6 +15,7 @@
 PY = 104
 PX = 104
 WIDE = 4
+INNER = 8
 PARTS = 8
 CHUNK = 512 // PARTS
 
@@ -311,8 +312,8 @@
         return remote(raw_a.at[1, pl.ds(pl.multiple_of(CHUNK * row, CHUNK), CHUNK), :], ysecond.at[d], dsend.at[d - 1],
                       drecv.at[d - 1], device(xh, row, core, z, xl))
 
-    def across(f, slot, x):
-        for h in range(0, WIDE, 2):
+    def across(f, slot, x, width):
+        for h in range(0, width, 2):
             u = fields[f][slot][pl.ds(4 + x + h, 2), pl.ds(0, NY), :]
             high = u.astype(jnp.bfloat16)
             low = (u - high.astype(jnp.float32)).astype(jnp.bfloat16)
@@ -333,47 +334,50 @@
         wait(f, slot_of(n - 1), (n - 1) % 2)
         amp = jnp.broadcast_to(extra[pl.ds(192, 8), pl.ds(n - 1, 1)], (8, NZ))
 
-        def planes(i, carry):
-            x = WIDE * i
+        def planes(x, width):
             if f == 0 and n > 1:
-                across(1, slot_of(n - 1), x)
+                across(1, slot_of(n - 1), x, width)
             if f == 1 and n < 8:
-                across(0, slot_of(n), x)
+                across(0, slot_of(n), x, width)
             for j in range(NY // 8):
                 rows = pl.ds(8 * j, 8)
-                wide = cur[pl.ds(x, WIDE + 8), rows, :]
-                u = wide[4:4 + WIDE]
-                acc = Z[f][pl.ds(x, WIDE), rows, :]
+                wide = cur[pl.ds(x, width + 8), rows, :]
+                u = wide[4:4 + width]
+                acc = Z[f][pl.ds(x, width), rows, :]
                 for k in range(1, 5):
-                    acc = acc + WEIGHTS[k] * (wide[4 + k:4 + k + WIDE] + wide[4 - k:4 - k + WIDE])
-                v = prev[pl.ds(4 + x, WIDE), rows, :]
+                    acc = acc + WEIGHTS[k] * (wide[4 + k:4 + k + width] + wide[4 - k:4 - k + width])
+                v = prev[pl.ds(4 + x, width), rows, :]
                 if f == 0:
-                    force = E[pl.ds(x, WIDE), rows, :] * amp[None]
+                    force = E[pl.ds(x, width), rows, :] * amp[None]
                 else:
-                    force = jnp.stack([pltpu.roll(T[x + h, rows, :], NZ - (8 - n), 1) * plane for h in range(WIDE)])
-                w = v + A[pl.ds(x, WIDE), rows, :] * ((u - v) + (C[pl.ds(x, WIDE), rows, :] * acc + force))
-                new[pl.ds(4 + x, WIDE), rows, :] = w
+                    force = jnp.stack([pltpu.roll(T[x + h, rows, :], NZ - (8 - n), 1) * plane for h in range(width)])
+                w = v + A[pl.ds(x, width), rows, :] * ((u - v) + (C[pl.ds(x, width), rows, :] * acc + force))
+                new[pl.ds(4 + x, width), rows, :] = w
                 if other is not None:
-                    image[pl.ds(x, WIDE), j // 2, pl.ds(8 * (j % 2), 8), :] += w * other[pl.ds(4 + x, WIDE), rows, :]
-            return carry
+                    image[pl.ds(x, width), j // 2, pl.ds(8 * (j % 2), 8), :] += w * other[pl.ds(4 + x, width), rows, :]
 
         if f == 1 and n == 8:
             for i in range(PARTS):
-                planes(i, 0)
+                planes(WIDE * i, WIDE)
                 if i == 0:
                     send_first()
                 else:
                     send_image(i)
             return
-        parts = [(0, 4 // WIDE, 0), (28 // WIDE, 32 // WIDE, 1), (4 // WIDE, 28 // WIDE, None)]
-        for first, last, side in parts:
-            lax.fori_loop(first, last, planes, 0)
-            if side is not None and n < 8:
+        for x0, side in ((0, 0), (28, 1)):
+            planes(x0, 4)
+            if n < 8:
                 send(f, slot_of(n), n % 2, side)
+
+        def inner(i, carry):
+            planes(4 + INNER * i, INNER)
+            return carry
+
+        lax.fori_loop(0, 24 // INNER, inner, 0)
 
     def first_across(f):
         def planes(i, carry):
-            across(f, 1, WIDE * i)
+            across(f, 1, WIDE * i, WIDE)
             return carry
         lax.fori_loop(0, NX // WIDE, planes, 0)
 

time: 156 us -> 155 us (level)
  Pallas kernels: 153 us -> 151 us
where the time goes in v7:
time: 155 us; the launch traced here: 154 us
  Pallas kernels  151 us (97%)
  local copies, waits for them, and re-layouts  1.67 us (1%)
    pallas_call x1, Pallas kernels, run_wave(): pl.pallas_call(wave_kernel, out_shape=jax.ShapeDtypeStruct((512, NZ), jnp...  151 us

profile of v7, /device:TPU:65, one launch (start us, length us, event | category | flops | bytes accessed | tf_op | source)
XLA Modules:
  0.0 154.4 jit_solution(7900171429854425490)
XLA Ops:
  1.3 151.4 %wave_steps.1 = f32[512,128]{1,0:T(8,128)} custom-call(s32[16]{0:T(128)} %blocks.1, f32[1,8]{1,0:T(1,128)} %wavelet.1, s32[1]{0:T(128)S(6)} %copy.13.cell_in, s32[1]{0:T(128)S(6)} %copy.14.depth_in, f32[512,128]{1,0:T(8,128)} %bitcast.11, f32[512,128]{1,0:T(8,128)} %bitcast.12, f32[2,3072,128]{2,1,0:T(8,128)} %bitcast.8, f32[2,3072,128]{2,1,0:T(8,128)} %bitcast.9, ...), custom_call_target="tpu_custom_call" | custom-call | tf_op jit(solution)/shard_map/wave_steps/pallas_call | solution.py:498
  152.7 1.7 %copy.15 = f32[16,32,128]{2,1,0:T(8,128)} copy(f32[16,32,128]{2,1,0:T(8,128)} %bitcast.10) | data formatting | bytes 524288
